TPU v7x, 256 devices: a whole 4x4x8 slice. The times are simulated.
256 devices in a mesh: lon: 16 (over y_lo, x, core), lat: 16 (over y_hi, z).
Axes of the slice: x: 4, y: 4 (y_hi: 2, y_lo: 2; y = y_hi * 2 + y_lo), z: 8, core: 2. Of those that a mesh axis runs over, the one named last changes fastest.
Arguments:
- tokens: bfloat16 [2, 192, 384, 192], P(None, 'lat', 'lon'), may hold values from -6 to 6
- gain_attn_first: float32 [192], replicated, may hold values from 0.1 to 1.9
- qkv_first: bfloat16 [192, 576], replicated, may hold values from -0.4375 to 0.4375
- proj_first: bfloat16 [192, 192], replicated, may hold values from -0.4375 to 0.4375
- gain_mlp_first: float32 [192], replicated, may hold values from 0.1 to 1.9
- up_first: bfloat16 [192, 768], replicated, may hold values from -0.4375 to 0.4375
- down_first: bfloat16 [768, 192], replicated, may hold values from -0.21875 to 0.21875
- bias_first: bfloat16 [32, 1, 6, 144, 144], P('lat'), may hold values from -6 to 6
- gain_attn_second: float32 [192], replicated, may hold values from 0.1 to 1.9
- qkv_second: bfloat16 [192, 576], replicated, may hold values from -0.4375 to 0.4375
- proj_second: bfloat16 [192, 192], replicated, may hold values from -0.4375 to 0.4375
- gain_mlp_second: float32 [192], replicated, may hold values from 0.1 to 1.9
- up_second: bfloat16 [192, 768], replicated, may hold values from -0.4375 to 0.4375
- down_second: bfloat16 [768, 192], replicated, may hold values from -0.21875 to 0.21875
- bias_second: bfloat16 [32, 1, 6, 144, 144], P('lat'), may hold values from -6 to 6
- cotangent: bfloat16 [2, 192, 384, 192], P(None, 'lat', 'lon'), may hold values from -6 to 6
Outputs:
- result: bfloat16 [2, 192, 384, 192], P(None, 'lat', 'lon')
- grad_tokens: bfloat16 [2, 192, 384, 192], P(None, 'lat', 'lon')
- grad_qkv_first: float32 [192, 576], replicated
- grad_proj_first: float32 [192, 192], replicated
- grad_up_first: float32 [192, 768], replicated
- grad_down_first: float32 [768, 192], replicated
- grad_qkv_second: float32 [192, 576], replicated
- grad_proj_second: float32 [192, 192], replicated
- grad_up_second: float32 [192, 768], replicated
- grad_down_second: float32 [768, 192], replicated
All inputs are finite; a program needn't handle non-finite values.
Results may differ from a plain program's by a relative error of at most 0.025.
Values may be sent and summed in bfloat16 or wider, within the bound.
A program may use at most 128 MiB of HBM per device.

v0:
```python
import functools
import math

import jax
import jax.numpy as jnp
from jax import lax
from jax.experimental import pallas as pl
from jax.experimental.pallas import tpu as pltpu
from jax.sharding import PartitionSpec as P

F32 = jnp.float32
BF16 = jnp.bfloat16
HEADS = 6
WIN = 144
PAD = 11
D = 192
STACK = 896
SCALE = 32 ** -0.5
CHUNKS = ((0, 256), (256, 512), (512, 768), (768, 896))
PIECE = 112
HALF = 16 * PIECE
ROWS = 2 * HALF
MESH = pl.DeviceIdType.MESH


def dot_nn(a, b):
    return lax.dot_general(a, b, (((1,), (0,)), ((), ())), preferred_element_type=F32)


def dot_nt(a, b):
    return lax.dot_general(a, b, (((1,), (1,)), ((), ())), preferred_element_type=F32)


def dot_tn(a, b):
    return lax.dot_general(a, b, (((0,), (0,)), ((), ())), preferred_element_type=F32)


def win_rows(w):
    return pl.ds(pl.multiple_of(w * WIN, 16), WIN)


def normalise(x):
    mean = jnp.mean(x, axis=-1, keepdims=True)
    centred = x - mean
    var = jnp.mean(centred * centred, axis=-1, keepdims=True)
    r = lax.rsqrt(var + 1e-05)
    return centred * r, r


def normalise_back(dy, xhat, r):
    m1 = jnp.mean(dy, axis=-1, keepdims=True)
    m2 = jnp.mean(dy * xhat, axis=-1, keepdims=True)
    return r * (dy - m1 - xhat * m2)


def live_column(first_row, limit):
    n = lax.broadcasted_iota(jnp.int32, (WIN, 1), 0)
    m = jnp.where(n >= 72, n - 72, n)
    row = jnp.zeros_like(m)
    for i in range(1, 6):
        row = row + jnp.where(m >= 12 * i, 1, 0)
    pos = row + first_row
    return jnp.where((pos >= 0) & (pos < limit), 1.0, 0.0).astype(F32)


def head_mask(h, dtype):
    lane = lax.broadcasted_iota(jnp.int32, (1, D), 1)
    inside = (lane >= 32 * h) & (lane < 32 * h + 32)
    return jnp.where(inside, 1.0, 0.0).astype(F32).astype(dtype)


def tile_to_windows(src, dst):
    for level in range(2):
        for row in range(12):
            x = src[level * 12 + row].astype(F32)
            for wc in range(2):
                at = ((row // 6) * 2 + wc) * WIN + level * 72 + (row % 6) * 12
                dst[at : at + 12, :] = x[12 * wc : 12 * wc + 12, :]


def windows_to_tile(src, dst):
    for level in range(2):
        for row in range(12):
            parts = []
            for wc in range(2):
                at = ((row // 6) * 2 + wc) * WIN + level * 72 + (row % 6) * 12
                parts.append(src[at : at + 12, :])
            dst[level * 12 + row] = jnp.concatenate(parts, axis=0).astype(BF16)


def place(level, row, col):
    return ((row // 6) * 2 + col // 12) * WIN + level * 72 + (row % 6) * 12 + col % 12


def pack_halo(src, pack, out, row0, row1, col0, col1):
    at = 0
    for rows, cols in ((row0, col1), (row1, col0), (row1, col1)):
        for level in range(2):
            for row in rows:
                for col in cols:
                    p = place(level, row, col)
                    pack[at : at + 6, :] = src[p : p + 6, :]
                    at += 6
        at = (at + 15) // 16 * 16
    out[...] = pack[...].astype(BF16)


HALO_ROWS = 112 + 112 + 48
HALO_PARTS = ((0, 112), (112, 112), (224, 48))


def unpack_shift(src, halo, dst, step):
    for level in range(2):
        for row in range(12):
            for col in range(0, 24, 6):
                r, c = row - 3 * step, col - 6 * step
                r_in, c_in = 0 <= r < 12, 0 <= c < 24
                if r_in and c_in:
                    p = place(level, r, c)
                    piece = src[p : p + 6, :]
                else:
                    if r_in:
                        i = r if step > 0 else r - 3
                        at = (level * 9 + i) * 6
                    elif c_in:
                        i = row if step > 0 else row - 9
                        j = c if step > 0 else c - 6
                        at = 112 + (level * 3 + i) * 18 + j
                    else:
                        i = row if step > 0 else row - 9
                        at = 224 + (level * 3 + i) * 6
                    piece = halo[at : at + 6, :]
                q = place(level, row, col)
                dst[q : q + 6, :] = piece


def megakernel(
    tok, ct,
    ga1, qkv1, proj1, gm1, up1, dn1, bias1,
    ga2, qkv2, proj2, gm2, up2, dn2, bias2,
    res_o, gt_o, f_o,
    wp, bt, xhat1, r1, normed, proj_all, qm, pt, att, xhat2, r2, second, hidden, gp,
    cur, nxt, cw, pack, halo_f, halo_out, halo_in,
    dtot, du, dres, dres_b, datt, dom, dst_, dqkv, w6,
    g, r0, hh, rr1, z, rr2, zg, f,
    halo_send, halo_recv, core_send, core_recv, xy_send, xy_recv, z_send, z_recv,
    zg_send, zg_recv, ag_send, ag_recv, fw_send, fw_recv, out_sem,
):
    lon = lax.axis_index("lon")
    lat = lax.axis_index("lat")
    core = lax.rem(lon, 2)
    chip = lon // 2
    y_hi = lat // 8
    zi = lax.rem(lat, 8)
    me_xy = y_hi * 8 + chip

    def sibling():
        return {"lon": chip * 2 + 1 - core, "lat": lat}

    def xy_dev(j):
        return {"lon": lax.rem(j, 8) * 2 + core, "lat": (j // 8) * 8 + zi}

    def z_dev(j):
        return {"lon": lon, "lat": y_hi * 8 + j}

    def near(step_lon, step_lat):
        return {
            "lon": lax.rem(lon + step_lon + 16, 16),
            "lat": lax.rem(lat + step_lat + 16, 16),
        }

    barrier = pltpu.get_barrier_semaphore()

    def greet(device):
        pl.semaphore_signal(barrier, inc=1, device_id=device, device_id_type=MESH)

    greet(sibling())
    for k in range(1, 16):
        greet(xy_dev(lax.rem(me_xy + k, 16)))
    for k in range(1, 8):
        greet(z_dev(lax.rem(zi + k, 8)))
    for s in (1, -1):
        greet(near(s, 0))
        greet(near(0, s))
        greet(near(s, s))

    def halo_copy(x, part, step):
        first, count = HALO_PARTS[part]
        device = near(step if part != 1 else 0, step if part != 0 else 0)
        return pltpu.make_async_remote_copy(
            src_ref=halo_out.at[x, pl.ds(first, count)],
            dst_ref=halo_in.at[x, pl.ds(first, count)],
            send_sem=halo_send.at[x, part],
            recv_sem=halo_recv.at[x, part],
            device_id=device,
            device_id_type=MESH,
        )

    def halo_start(x, src, step):
        if step > 0:
            pack_halo(src, pack, halo_out.at[x], range(0, 9), range(9, 12), (0, 6, 12), (18,))
        else:
            pack_halo(src, pack, halo_out.at[x], range(3, 12), range(0, 3), (6, 12, 18), (0,))
        for part in range(3):
            halo_copy(x, part, step).start()

    def halo_finish(x, src, dst, step):
        for part in range(3):
            halo_copy(x, part, step).wait()
        outside = jnp.where(lat == (0 if step > 0 else 15), 0.0, 1.0).astype(F32)
        halo_f[0:112, :] = halo_in[x, 0:112].astype(F32)
        halo_f[112:, :] = halo_in[x, 112:].astype(F32) * outside
        unpack_shift(src, halo_f, dst, step)

    limit = 16 * 12 - PAD
    starts = (lat * 12, lat * 12 - 3)
    weights = (
        (ga1, qkv1, proj1, gm1, up1, dn1, bias1),
        (ga2, qkv2, proj2, gm2, up2, dn2, bias2),
    )

    def live(b, w):
        return live_column(starts[b] + 6 * (w // 2), limit)

    def block_forward(b, x_in, x_out):
        ga, wqkv, wproj, gm, wup, wdn, bias = weights[b]
        wp[b] = jnp.zeros((D, 768), BF16)
        for i in range(3):
            part = wqkv[...].astype(F32)[:, D * i : D * i + D]
            wp[b, :, 256 * i : 256 * i + D] = part.astype(BF16)
        rows_i = lax.broadcasted_iota(jnp.int32, (WIN, WIN), 0)
        cols_i = lax.broadcasted_iota(jnp.int32, (WIN, WIN), 1)
        eye = jnp.where(rows_i == cols_i, 1.0, 0.0).astype(F32).astype(BF16)
        for wr in range(2):
            penalty = (live_column(starts[b] + 6 * wr, limit) - 1.0) * 30000.0
            bt[wr, :, 0:864] = dot_nt(eye, bias[wr]) + penalty
            bt[wr, :, 864:] = jnp.zeros((WIN, STACK - 864), F32)
        gain_a = ga[...].reshape(1, D)
        gain_m = gm[...].reshape(1, D)

        @pl.loop(0, 4)
        def _(w):
            rows = win_rows(w)
            xh, r = normalise(x_in[rows, :])
            xhat1[b, rows, :] = xh
            r1[b, rows, :] = r
            nb = (xh * gain_a).astype(BF16)
            normed[b, rows, :] = nb
            proj_all[b, rows, :] = dot_nn(nb, wp[b]).astype(BF16)

        @pl.loop(0, 4)
        def _(w):
            rows = win_rows(w)
            wr = w // 2
            q = proj_all[b, rows, 0:D]
            k = proj_all[b, rows, 256 : 256 + D]
            v = proj_all[b, rows, 512 : 512 + D]
            for h in range(HEADS):
                qm[b, w, WIN * h : WIN * h + WIN, :] = q * head_mask(h, BF16)
            qm[b, w, 864:, :] = jnp.zeros((STACK - 864, D), BF16)
            for c0, c1 in CHUNKS:
                s = dot_nt(k, qm[b, w, c0:c1, :]) * SCALE + bt[wr, :, c0:c1]
                e = jnp.exp(s - jnp.max(s, axis=0, keepdims=True))
                total = jnp.sum(e, axis=0, keepdims=True)
                pt[b, w, :, c0:c1] = (e * (1.0 / total)).astype(BF16)
            o = dot_tn(pt[b, w], v)
            a = jnp.zeros((WIN, D), F32)
            for h in range(HEADS):
                a = a + o[WIN * h : WIN * h + WIN, :] * head_mask(h, F32)
            att[b, rows, :] = a.astype(BF16)

        @pl.loop(0, 4)
        def _(w):
            rows = win_rows(w)
            resid = x_in[rows, :] + dot_nn(att[b, rows, :], wproj[...])
            xh, r = normalise(resid)
            xhat2[b, rows, :] = xh
            r2[b, rows, :] = r
            sb = (xh * gain_m).astype(BF16)
            second[b, rows, :] = sb
            u = dot_nn(sb, wup[...])
            c = math.sqrt(2.0 / math.pi)
            u2 = u * u
            t = jnp.tanh(u * (c + (c * 0.044715) * u2))
            half = 0.5 + 0.5 * t
            hb = (u * half).astype(BF16)
            hidden[b, rows, :] = hb
            slope = half + u * (0.5 - 0.5 * t * t) * (c + (3 * c * 0.044715) * u2)
            gp[b, rows, :] = slope.astype(BF16)
            out = (resid + dot_nn(hb, wdn[...])) * live(b, w)
            x_out[rows, :] = out.astype(BF16).astype(F32)

    def block_backward(b, d_out, d_in):
        ga, wqkv, wproj, gm, wup, wdn, bias = weights[b]
        gain_a = ga[...].reshape(1, D)
        gain_m = gm[...].reshape(1, D)

        @pl.loop(0, 4)
        def _(w):
            rows = win_rows(w)
            dt = d_out[rows, :] * live(b, w)
            dtb = dt.astype(BF16)
            dtot[rows, :] = dtb
            dh = dot_nt(dtb, wdn[...]).astype(BF16).astype(F32)
            dub = (dh * gp[b, rows, :].astype(F32)).astype(BF16)
            du[rows, :] = dub
            dy = dot_nt(dub, wup[...]).astype(BF16).astype(F32) * gain_m
            dr = dt + normalise_back(dy, xhat2[b, rows, :], r2[b, rows, :])
            dres[rows, :] = dr
            drb = dr.astype(BF16)
            dres_b[rows, :] = drb
            datt[rows, :] = dot_nt(drb, wproj[...]).astype(BF16)

        @pl.loop(0, 4)
        def _(w):
            rows = win_rows(w)
            k = proj_all[b, rows, 256 : 256 + D]
            v = proj_all[b, rows, 512 : 512 + D]
            do = datt[rows, :]
            for h in range(HEADS):
                dom[WIN * h : WIN * h + WIN, :] = do * head_mask(h, BF16)
            dom[864:, :] = jnp.zeros((STACK - 864, D), BF16)
            for c0, c1 in CHUNKS:
                dp = dot_nt(v, dom[c0:c1, :]).astype(BF16).astype(F32)
                p = pt[b, w, :, c0:c1].astype(F32)
                delta = jnp.sum(p * dp, axis=0, keepdims=True)
                dst_[:, c0:c1] = (p * (dp - delta)).astype(BF16)
            zeros = jnp.zeros((WIN, 64), BF16)
            dqkv[rows, 512 : 512 + D] = dot_nn(pt[b, w], dom[...]).astype(BF16)
            dqkv[rows, 256 : 256 + D] = (dot_nn(dst_[...], qm[b, w]) * SCALE).astype(BF16)
            o = dot_tn(dst_[...], k)
            a = jnp.zeros((WIN, D), F32)
            for h in range(HEADS):
                a = a + o[WIN * h : WIN * h + WIN, :] * head_mask(h, F32)
            dqkv[rows, 0:D] = (a * SCALE).astype(BF16)
            for i in range(3):
                dqkv[rows, 256 * i + D : 256 * i + 256] = zeros

        @pl.loop(0, 4)
        def _(w):
            rows = win_rows(w)
            dy = dot_nt(dqkv[rows, :], wp[b]).astype(BF16).astype(F32) * gain_a
            dx = dres[rows, :] + normalise_back(dy, xhat1[b, rows, :], r1[b, rows, :])
            d_in[rows, :] = dx.astype(BF16).astype(F32)

    def weight_terms(b):
        w6[...] = dot_tn(normed[b], dqkv[...])
        pr = dot_tn(att[b], dres_b[...])
        for i in range(3):
            w6[:, 256 * i + D : 256 * i + 256] = pr[:, 64 * i : 64 * i + 64]
        for i in range(6):
            g[b, i * D : i * D + D, :] = w6[:, 128 * i : 128 * i + 128].astype(BF16)
        gu = dot_tn(second[b], du[...])
        for i in range(6):
            g[b, (6 + i) * D : (7 + i) * D, :] = gu[:, 128 * i : 128 * i + 128].astype(BF16)
        gd = dot_tn(dtot[...], hidden[b])
        for i in range(6):
            g[b, (12 + i) * D : (13 + i) * D, :] = gd[:, 128 * i : 128 * i + 128].astype(BF16)
        g[b, 18 * D :, :] = jnp.zeros((ROWS - 18 * D, 128), BF16)

    def remote(src, dst, send, recv, device):
        return pltpu.make_async_remote_copy(
            src_ref=src, dst_ref=dst, send_sem=send, recv_sem=recv,
            device_id=device, device_id_type=MESH,
        )

    def half_at(c):
        return pl.ds(pl.multiple_of(c * HALF, 16), HALF)

    def piece_at(j):
        return pl.ds(pl.multiple_of(j * PIECE, 16), PIECE)

    def f_at(j):
        return pl.ds(pl.multiple_of(core * HALF + j * PIECE, 16), PIECE)

    def tile_at(j):
        return pl.ds(pl.multiple_of(j * 16, 16), 16)

    def core_copy(b):
        return remote(g.at[b, half_at(1 - core)], r0.at[b], core_send.at[b], core_recv.at[b], sibling())

    def xy_copy(b, j, slot):
        return remote(hh.at[b, piece_at(j)], rr1.at[b, slot], xy_send.at[b, j], xy_recv.at[b, slot], xy_dev(j))

    def z_copy(b, j, slot):
        return remote(z.at[b, tile_at(j)], rr2.at[b, slot], z_send.at[b, j], z_recv.at[b, slot], z_dev(j))

    def zg_copy(b, j, slot):
        return remote(zg.at[b, tile_at(slot)], zg.at[b, tile_at(slot)], zg_send.at[b, j], zg_recv.at[b, slot], z_dev(j))

    def ag_copy(b, j, slot):
        return remote(f.at[b, f_at(slot)], f.at[b, f_at(slot)], ag_send.at[b, j], ag_recv.at[b, slot], xy_dev(j))

    def fw_copy(b, j):
        return remote(f.at[b, f_at(j)], f.at[b, f_at(j)], fw_send.at[b, j], fw_recv.at[b, j], sibling())

    def fw_arrived(b, j):
        other = pl.ds(pl.multiple_of((1 - core) * HALF + j * PIECE, 16), PIECE)
        return remote(f.at[b, other], f.at[b, other], fw_send.at[b, j], fw_recv.at[b, j], sibling())

    def xy_others(body):
        def step(k, carry):
            body(lax.rem(me_xy + k, 16))
            return carry
        lax.fori_loop(1, 16, step, 0)

    def z_others(body):
        def step(k, carry):
            body(lax.rem(zi + k, 8))
            return carry
        lax.fori_loop(1, 8, step, 0)

    def sum_0(b):
        core_copy(b).start()

    def sum_1(b):
        core_copy(b).wait()
        def step(j, carry):
            own = g[b, pl.ds(pl.multiple_of(core * HALF + j * PIECE, 16), PIECE), :].astype(F32)
            hh[b, piece_at(j), :] = (own + r0[b, piece_at(j), :].astype(F32)).astype(BF16)
            return carry
        lax.fori_loop(0, 16, step, 0)
        xy_others(lambda j: xy_copy(b, j, me_xy).start())

    def sum_2(b):
        xy_others(lambda j: xy_copy(b, me_xy, j).wait_recv())
        rr1[b, me_xy] = hh[b, piece_at(me_xy), :]
        total = lax.fori_loop(
            0, 16, lambda j, a: a + rr1[b, j].astype(F32), jnp.zeros((PIECE, 128), F32)
        )
        z[b, 0:PIECE, :] = total.astype(BF16)
        z[b, PIECE:, :] = jnp.zeros((16, 128), BF16)
        z_others(lambda j: z_copy(b, j, zi).start())

    def sum_3(b):
        z_others(lambda j: z_copy(b, zi, j).wait_recv())
        rr2[b, zi] = z[b, tile_at(zi), :]
        total = jnp.zeros((16, 128), F32)
        for j in range(8):
            total = total + rr2[b, j].astype(F32)
        zg[b, tile_at(zi), :] = total.astype(BF16)
        z_others(lambda j: zg_copy(b, j, zi).start())

    def sum_4(b):
        z_others(lambda j: zg_copy(b, zi, j).wait_recv())
        f[b, f_at(me_xy), :] = zg[b, 0:PIECE, :]
        xy_others(lambda j: ag_copy(b, j, me_xy).start())
        fw_copy(b, me_xy).start()

    def sum_5(b):
        def forward(j):
            ag_copy(b, me_xy, j).wait_recv()
            fw_copy(b, j).start()
        xy_others(forward)

    def sum_6(b):
        def arrived(j, carry):
            fw_arrived(b, j).wait_recv()
            fw_copy(b, j).wait_send()
            return carry
        lax.fori_loop(0, 16, arrived, 0)
        def sent(j):
            xy_copy(b, j, me_xy).wait_send()
            ag_copy(b, j, me_xy).wait_send()
        xy_others(sent)
        def sent_z(j):
            z_copy(b, j, zi).wait_send()
            zg_copy(b, j, zi).wait_send()
        z_others(sent_z)

    tile_to_windows(tok, cur)
    tile_to_windows(ct, cw)
    pl.semaphore_wait(barrier, 29)
    halo_start(0, cw, 1)
    block_forward(0, cur, nxt)
    halo_start(1, nxt, 1)
    halo_finish(1, nxt, cur, 1)
    block_forward(1, cur, nxt)
    halo_start(2, nxt, -1)
    halo_finish(0, cw, cur, 1)
    block_backward(1, cur, cw)
    halo_start(3, cw, -1)
    weight_terms(1)
    sum_0(1)
    halo_finish(2, nxt, cur, -1)
    windows_to_tile(cur, res_o)
    halo_finish(3, cw, nxt, -1)
    block_backward(0, nxt, cur)
    weight_terms(0)
    windows_to_tile(cur, gt_o)
    sum_0(0)
    sum_1(1)
    sum_1(0)
    sum_2(1)
    sum_2(0)
    sum_3(1)
    sum_3(0)
    sum_4(1)
    sum_4(0)
    sum_5(1)
    sum_5(0)
    sum_6(1)
    sum_6(0)
    out = pltpu.make_async_copy(f, f_o, out_sem)
    out.start()
    out.wait()


def unpack_kernel(factor, f, res, gt, res_o, gt_o, *outs):
    res_o[...] = res[...]
    gt_o[...] = gt[...]
    for b in range(2):
        qkv, proj, up, down = outs[4 * b : 4 * b + 4]

        def tile(i):
            return f[b, i * D : i * D + D, :].astype(F32) * factor

        for i in range(3):
            two = jnp.concatenate([tile(2 * i), tile(2 * i + 1)], axis=1)
            qkv[:, D * i : D * i + D] = two[:, 0:D]
            proj[:, 64 * i : 64 * i + 64] = two[:, D:]
        for i in range(6):
            up[:, 128 * i : 128 * i + 128] = tile(6 + i)
            down[128 * i : 128 * i + 128, :] = tile(12 + i).T


def body(
    tokens, ga1, qkv1, proj1, gm1, up1, dn1, bias1,
    ga2, qkv2, proj2, gm2, up2, dn2, bias2, cotangent,
):
    vmem = pl.BlockSpec(memory_space=pltpu.VMEM)
    tile = jax.ShapeDtypeStruct((24, 24, D), BF16)

    def dma(*shape):
        return pltpu.SemaphoreType.DMA(shape)

    scratch = [
        pltpu.VMEM((2, D, 768), BF16),
        pltpu.VMEM((2, WIN, STACK), F32),
        pltpu.VMEM((2, 576, D), F32),
        pltpu.VMEM((2, 576, 1), F32),
        pltpu.VMEM((2, 576, D), BF16),
        pltpu.VMEM((2, 576, 768), BF16),
        pltpu.VMEM((2, 4, STACK, D), BF16),
        pltpu.VMEM((2, 4, WIN, STACK), BF16),
        pltpu.VMEM((2, 576, D), BF16),
        pltpu.VMEM((2, 576, D), F32),
        pltpu.VMEM((2, 576, 1), F32),
        pltpu.VMEM((2, 576, D), BF16),
        pltpu.VMEM((2, 576, 768), BF16),
        pltpu.VMEM((2, 576, 768), BF16),
        pltpu.VMEM((576, D), F32),
        pltpu.VMEM((576, D), F32),
        pltpu.VMEM((576, D), F32),
        pltpu.VMEM((HALO_ROWS, D), F32),
        pltpu.VMEM((HALO_ROWS, D), F32),
        pltpu.VMEM((4, HALO_ROWS, D), BF16),
        pltpu.VMEM((4, HALO_ROWS, D), BF16),
        pltpu.VMEM((576, D), BF16),
        pltpu.VMEM((576, 768), BF16),
        pltpu.VMEM((576, D), F32),
        pltpu.VMEM((576, D), BF16),
        pltpu.VMEM((576, D), BF16),
        pltpu.VMEM((STACK, D), BF16),
        pltpu.VMEM((WIN, STACK), BF16),
        pltpu.VMEM((576, 768), BF16),
        pltpu.VMEM((D, 768), F32),
        pltpu.VMEM((2, ROWS, 128), BF16),
        pltpu.VMEM((2, HALF, 128), BF16),
        pltpu.VMEM((2, HALF, 128), BF16),
        pltpu.VMEM((2, 16, PIECE, 128), BF16),
        pltpu.VMEM((2, 128, 128), BF16),
        pltpu.VMEM((2, 8, 16, 128), BF16),
        pltpu.VMEM((2, 128, 128), BF16),
        pltpu.VMEM((2, ROWS, 128), BF16),
        dma(4, 3), dma(4, 3),
        dma(2), dma(2),
        dma(2, 16), dma(2, 16),
        dma(2, 8), dma(2, 8),
        dma(2, 8), dma(2, 8),
        dma(2, 16), dma(2, 16),
        dma(2, 16), dma(2, 16),
        pltpu.SemaphoreType.DMA,
    ]
    res, gt, f = pl.pallas_call(
        megakernel,
        out_shape=(tile, tile, jax.ShapeDtypeStruct((2, ROWS, 128), BF16)),
        in_specs=[vmem] * 16,
        out_specs=(vmem, vmem, pl.BlockSpec(memory_space=pl.ANY)),
        scratch_shapes=scratch,
        compiler_params=pltpu.CompilerParams(
            collective_id=0, has_side_effects=True, vmem_limit_bytes=56 * 1024 * 1024
        ),
    )(
        tokens.reshape(24, 24, D), cotangent.reshape(24, 24, D),
        ga1, qkv1, proj1, gm1, up1, dn1, bias1.reshape(2, HEADS * WIN, WIN),
        ga2, qkv2, proj2, gm2, up2, dn2, bias2.reshape(2, HEADS * WIN, WIN),
    )
    one = [
        jax.ShapeDtypeStruct((D, 3 * D), F32),
        jax.ShapeDtypeStruct((D, D), F32),
        jax.ShapeDtypeStruct((D, 4 * D), F32),
        jax.ShapeDtypeStruct((4 * D, D), F32),
    ]
    outs = pl.pallas_call(
        functools.partial(unpack_kernel, 1.0 / math.sqrt(256.0 * 576.0)),
        out_shape=[tile, tile] + one + one,
        in_specs=[vmem] * 3,
        out_specs=[vmem] * 10,
        compiler_params=pltpu.CompilerParams(vmem_limit_bytes=48 * 1024 * 1024),
    )(f, res, gt)
    shape = (2, 12, 24, D)
    return (outs[0].reshape(shape), outs[1].reshape(shape)) + tuple(outs[2:])


def solution(mesh):
    grid = P(None, "lat", "lon", None)
    bias = P("lat", None, None, None, None)
    block = (P(), P(), P(), P(), P(), P(), bias)
    return jax.shard_map(
        body,
        mesh=mesh,
        in_specs=(grid,) + block + block + (grid,),
        out_specs=(grid, grid) + (P(),) * 8,
        check_vma=False,
    )
```

profile of v0, /device:TPU:1, one launch (start us, length us, event | category | flops | bytes accessed | tf_op | source)
XLA Modules:
  0.0 103.3 jit_solution(5853677099911920282)
XLA Ops:
  0.6 1.9 %copy.26.dn1 = bf16[768,192]{1,0:T(8,128)(2,1)} copy(bf16[768,192]{0,1:T(8,128)(2,1)} %param.22) | data formatting | bytes 589824 | tf_op args[6]
  2.5 1.9 %copy.27.dn2 = bf16[768,192]{1,0:T(8,128)(2,1)} copy(bf16[768,192]{0,1:T(8,128)(2,1)} %param.29) | data formatting | bytes 589824 | tf_op args[13]
  4.4 91.1 %shard_map.231 = (bf16[24,24,192]{2,1,0:T(8,128)(2,1)}, bf16[24,24,192]{2,1,0:T(8,128)(2,1)}, bf16[2,3584,128]{2,1,0:T(8,128)(2,1)}) custom-call(bf16[24,24,192]{2,1,0:T(8,128)(2,1)} %bitcast.8, bf16[24,24,192]{2,1,0:T(8,128)(2,1)} %bitcast.9, f32[192]{0:T(256)} %ga1.1, bf16[192,576]{1,0:T(8,128)(2,1)} %qkv1.1, bf16[192,192]{1,0:T(8,128)(2,1)} %proj1.1, ...), custom_call_target="tpu_custom_call" | custom-call | tf_op jit(solution)/shard_map/pallas_call | solution.py:585
  95.5 0.0 copy-start
  95.5 1.5 %copy-done = bf16[2,3584,128]{2,1,0:T(8,128)(2,1)S(1)} copy-done((bf16[2,3584,128]{2,1,0:T(8,128)(2,1)S(1)}, bf16[2,3584,128]{2,1,0:T(8,128)(2,1)}, u32[]{:S(2)}) %copy-start) | copy-done | bytes 1835032
  97.0 0.0 copy-start.1
  97.0 1.0 copy-done.1
  97.9 0.0 copy-start.2
  97.9 1.0 copy-done.2
  98.9 2.2 %shard_map.232 = (bf16[24,24,192]{2,1,0:T(8,128)(2,1)}, bf16[24,24,192]{2,1,0:T(8,128)(2,1)}, f32[192,576]{1,0:T(8,128)}, f32[192,192]{1,0:T(8,128)}, f32[192,76...) custom-call(bf16[2,3584,128]{2,1,0:T(8,128)(2,1)S(1)} %copy-done, ...), custom_call_target="tpu_custom_call" | custom-call | tf_op jit(solution)/shard_map/pallas_call | solution.py:605
  101.1 1.1 %copy.28 = f32[768,192]{0,1:T(8,128)} copy(f32[768,192]{1,0:T(8,128)S(1)} %get-tuple-element.41) | data formatting | bytes 1179648
  102.2 1.1 %copy.29 = f32[768,192]{0,1:T(8,128)} copy(f32[768,192]{1,0:T(8,128)S(1)} %get-tuple-element.45) | data formatting | bytes 1179648
Async XLA Ops:
  95.5 1.5 %copy-start = (bf16[2,3584,128]{2,1,0:T(8,128)(2,1)S(1)}, bf16[2,3584,128]{2,1,0:T(8,128)(2,1)}, u32[]{:S(2)}) copy-start(bf16[2,3584,128]{2,1,0:T(8,128)(2,1)} %get-tuple-element.23.f) | copy-start | bytes 5505028
  97.0 1.0 copy-start.1
  97.9 1.0 copy-start.2
where the time goes:
time: 104 us; the launch traced here: 103 us
  Pallas kernels  93.3 us (90%)
  local copies, waits for them, and re-layouts  9.3 us (9%)
    pallas_call x1, Pallas kernels, body(): pl.pallas_call(megakernel, out_shape=(tile, tile, jax.ShapeDtypeStruct((2...  91.1 us
    unnamed x10, local copies, waits for them, and re-layouts  9.3 us
    pallas_call x1, Pallas kernels, body(): pl.pallas_call(functools.partial(unpack_kernel, 1.0 / math.sqrt(256.0 * 5...  2.23 us

commit v1 on v0

--- a/solution.py
+++ b/solution.py
@@ -17,9 +17,9 @@
 STACK = 896
 SCALE = 32 ** -0.5
 CHUNKS = ((0, 256), (256, 512), (512, 768), (768, 896))
-PIECE = 112
-HALF = 16 * PIECE
-ROWS = 2 * HALF
+PIECES = (112, 80, 48)
+BASES = (0, 32 * 112, 32 * 192)
+ROWS = 32 * 240
 MESH = pl.DeviceIdType.MESH
 
 
@@ -33,6 +33,10 @@
 
 def dot_tn(a, b):
     return lax.dot_general(a, b, (((0,), (0,)), ((), ())), preferred_element_type=F32)
+
+
+def stage(name, work):
+    work()
 
 
 def win_rows(w):
@@ -109,10 +113,12 @@
 HALO_PARTS = ((0, 112), (112, 112), (224, 48))
 
 
-def unpack_shift(src, halo, dst, step):
+def unpack_shift(src, halo, dst, step, windows):
     for level in range(2):
         for row in range(12):
             for col in range(0, 24, 6):
+                if (row // 6) * 2 + col // 12 not in windows:
+                    continue
                 r, c = row - 3 * step, col - 6 * step
                 r_in, c_in = 0 <= r < 12, 0 <= c < 24
                 if r_in and c_in:
@@ -140,12 +146,14 @@
     ga2, qkv2, proj2, gm2, up2, dn2, bias2,
     res_o, gt_o, f_o,
     wp, bt, xhat1, r1, normed, proj_all, qm, pt, att, xhat2, r2, second, hidden, gp,
-    cur, nxt, cw, pack, halo_f, halo_out, halo_in,
+    cur, nxt, out2, cw, pack, halo_f, halo_out, halo_in,
     dtot, du, dres, dres_b, datt, dom, dst_, dqkv, w6,
-    g, r0, hh, rr1, z, rr2, zg, f,
+    g_0, g_1, g_2, r_0, r_1, r_2, h_0, h_1, h_2, rr_0, rr_1, rr_2, z_0, z_1, z_2, f,
     halo_send, halo_recv, core_send, core_recv, xy_send, xy_recv, z_send, z_recv,
-    zg_send, zg_recv, ag_send, ag_recv, fw_send, fw_recv, out_sem,
+    ag_send, ag_recv, fw_send, fw_recv, out_sem,
 ):
+    gs, r0s, hhs = (g_0, g_1, g_2), (r_0, r_1, r_2), (h_0, h_1, h_2)
+    rrs, zs = (rr_0, rr_1, rr_2), (z_0, z_1, z_2)
     lon = lax.axis_index("lon")
     lat = lax.axis_index("lat")
     core = lax.rem(lon, 2)
@@ -204,13 +212,13 @@
         for part in range(3):
             halo_copy(x, part, step).start()
 
-    def halo_finish(x, src, dst, step):
+    def halo_finish(x, src, dst, step, windows=(0, 1, 2, 3)):
         for part in range(3):
             halo_copy(x, part, step).wait()
         outside = jnp.where(lat == (0 if step > 0 else 15), 0.0, 1.0).astype(F32)
         halo_f[0:112, :] = halo_in[x, 0:112].astype(F32)
         halo_f[112:, :] = halo_in[x, 112:].astype(F32) * outside
-        unpack_shift(src, halo_f, dst, step)
+        unpack_shift(src, halo_f, dst, step, windows)
 
     limit = 16 * 12 - PAD
     starts = (lat * 12, lat * 12 - 3)
@@ -222,7 +230,7 @@
     def live(b, w):
         return live_column(starts[b] + 6 * (w // 2), limit)
 
-    def block_forward(b, x_in, x_out):
+    def prepare(b):
         ga, wqkv, wproj, gm, wup, wdn, bias = weights[b]
         wp[b] = jnp.zeros((D, 768), BF16)
         for i in range(3):
@@ -235,11 +243,13 @@
             penalty = (live_column(starts[b] + 6 * wr, limit) - 1.0) * 30000.0
             bt[wr, :, 0:864] = dot_nt(eye, bias[wr]) + penalty
             bt[wr, :, 864:] = jnp.zeros((WIN, STACK - 864), F32)
+
+    def block_forward(b, x_in, x_out, lo, hi):
+        ga, wqkv, wproj, gm, wup, wdn, bias = weights[b]
         gain_a = ga[...].reshape(1, D)
         gain_m = gm[...].reshape(1, D)
 
-        @pl.loop(0, 4)
-        def _(w):
+        def f_qkv(w):
             rows = win_rows(w)
             xh, r = normalise(x_in[rows, :])
             xhat1[b, rows, :] = xh
@@ -248,8 +258,9 @@
             normed[b, rows, :] = nb
             proj_all[b, rows, :] = dot_nn(nb, wp[b]).astype(BF16)
 
-        @pl.loop(0, 4)
-        def _(w):
+        stage("f_qkv", lambda: pl.loop(lo, hi)(f_qkv))
+
+        def f_att(w):
             rows = win_rows(w)
             wr = w // 2
             q = proj_all[b, rows, 0:D]
@@ -269,8 +280,9 @@
                 a = a + o[WIN * h : WIN * h + WIN, :] * head_mask(h, F32)
             att[b, rows, :] = a.astype(BF16)
 
-        @pl.loop(0, 4)
-        def _(w):
+        stage("f_att", lambda: pl.loop(lo, hi)(f_att))
+
+        def f_mlp(w):
             rows = win_rows(w)
             resid = x_in[rows, :] + dot_nn(att[b, rows, :], wproj[...])
             xh, r = normalise(resid)
@@ -287,21 +299,21 @@
             hidden[b, rows, :] = hb
             slope = half + u * (0.5 - 0.5 * t * t) * (c + (3 * c * 0.044715) * u2)
             gp[b, rows, :] = slope.astype(BF16)
-            out = (resid + dot_nn(hb, wdn[...])) * live(b, w)
+            out = (resid + dot_nt(hb, wdn[...])) * live(b, w)
             x_out[rows, :] = out.astype(BF16).astype(F32)
 
-    def block_backward(b, d_out, d_in):
+        stage("f_mlp", lambda: pl.loop(lo, hi)(f_mlp))
+
+    def mlp_backward(b, d_out, lo, hi):
         ga, wqkv, wproj, gm, wup, wdn, bias = weights[b]
-        gain_a = ga[...].reshape(1, D)
         gain_m = gm[...].reshape(1, D)
 
-        @pl.loop(0, 4)
-        def _(w):
+        def b_mlp(w):
             rows = win_rows(w)
             dt = d_out[rows, :] * live(b, w)
             dtb = dt.astype(BF16)
             dtot[rows, :] = dtb
-            dh = dot_nt(dtb, wdn[...]).astype(BF16).astype(F32)
+            dh = dot_nn(dtb, wdn[...]).astype(BF16).astype(F32)
             dub = (dh * gp[b, rows, :].astype(F32)).astype(BF16)
             du[rows, :] = dub
             dy = dot_nt(dub, wup[...]).astype(BF16).astype(F32) * gain_m
@@ -311,8 +323,10 @@
             dres_b[rows, :] = drb
             datt[rows, :] = dot_nt(drb, wproj[...]).astype(BF16)
 
-        @pl.loop(0, 4)
-        def _(w):
+        stage("b_mlp", lambda: pl.loop(lo, hi)(b_mlp))
+
+    def attention_backward(b, lo, hi, between=None):
+        def b_att(w):
             rows = win_rows(w)
             k = proj_all[b, rows, 256 : 256 + D]
             v = proj_all[b, rows, 512 : 512 + D]
@@ -336,27 +350,36 @@
             for i in range(3):
                 dqkv[rows, 256 * i + D : 256 * i + 256] = zeros
 
-        @pl.loop(0, 4)
-        def _(w):
+            if between is not None:
+                between(w)
+
+        stage("b_att", lambda: pl.loop(lo, hi)(b_att))
+
+    def input_backward(b, d_in, lo, hi):
+        gain_a = weights[b][0][...].reshape(1, D)
+
+        def b_qkv(w):
             rows = win_rows(w)
             dy = dot_nt(dqkv[rows, :], wp[b]).astype(BF16).astype(F32) * gain_a
             dx = dres[rows, :] + normalise_back(dy, xhat1[b, rows, :], r1[b, rows, :])
             d_in[rows, :] = dx.astype(BF16).astype(F32)
 
-    def weight_terms(b):
+        stage("b_qkv", lambda: pl.loop(lo, hi)(b_qkv))
+
+    def put(gr, at, matrix):
+        for i in range(6):
+            gs[gr][at + i * D : at + i * D + D, :] = matrix[:, 128 * i : 128 * i + 128].astype(BF16)
+
+    def mlp_terms(b, gr, at):
+        put(gr, at, dot_tn(second[b], du[...]))
+        put(gr, at + 6 * D, dot_tn(dtot[...], hidden[b]))
+
+    def attention_terms(b, gr, at):
         w6[...] = dot_tn(normed[b], dqkv[...])
         pr = dot_tn(att[b], dres_b[...])
         for i in range(3):
             w6[:, 256 * i + D : 256 * i + 256] = pr[:, 64 * i : 64 * i + 64]
-        for i in range(6):
-            g[b, i * D : i * D + D, :] = w6[:, 128 * i : 128 * i + 128].astype(BF16)
-        gu = dot_tn(second[b], du[...])
-        for i in range(6):
-            g[b, (6 + i) * D : (7 + i) * D, :] = gu[:, 128 * i : 128 * i + 128].astype(BF16)
-        gd = dot_tn(dtot[...], hidden[b])
-        for i in range(6):
-            g[b, (12 + i) * D : (13 + i) * D, :] = gd[:, 128 * i : 128 * i + 128].astype(BF16)
-        g[b, 18 * D :, :] = jnp.zeros((ROWS - 18 * D, 128), BF16)
+        put(gr, at, w6)
 
     def remote(src, dst, send, recv, device):
         return pltpu.make_async_remote_copy(
@@ -364,39 +387,33 @@
             device_id=device, device_id_type=MESH,
         )
 
-    def half_at(c):
-        return pl.ds(pl.multiple_of(c * HALF, 16), HALF)
-
-    def piece_at(j):
-        return pl.ds(pl.multiple_of(j * PIECE, 16), PIECE)
-
-    def f_at(j):
-        return pl.ds(pl.multiple_of(core * HALF + j * PIECE, 16), PIECE)
-
-    def tile_at(j):
-        return pl.ds(pl.multiple_of(j * 16, 16), 16)
-
-    def core_copy(b):
-        return remote(g.at[b, half_at(1 - core)], r0.at[b], core_send.at[b], core_recv.at[b], sibling())
-
-    def xy_copy(b, j, slot):
-        return remote(hh.at[b, piece_at(j)], rr1.at[b, slot], xy_send.at[b, j], xy_recv.at[b, slot], xy_dev(j))
-
-    def z_copy(b, j, slot):
-        return remote(z.at[b, tile_at(j)], rr2.at[b, slot], z_send.at[b, j], z_recv.at[b, slot], z_dev(j))
-
-    def zg_copy(b, j, slot):
-        return remote(zg.at[b, tile_at(slot)], zg.at[b, tile_at(slot)], zg_send.at[b, j], zg_recv.at[b, slot], z_dev(j))
-
-    def ag_copy(b, j, slot):
-        return remote(f.at[b, f_at(slot)], f.at[b, f_at(slot)], ag_send.at[b, j], ag_recv.at[b, slot], xy_dev(j))
-
-    def fw_copy(b, j):
-        return remote(f.at[b, f_at(j)], f.at[b, f_at(j)], fw_send.at[b, j], fw_recv.at[b, j], sibling())
-
-    def fw_arrived(b, j):
-        other = pl.ds(pl.multiple_of((1 - core) * HALF + j * PIECE, 16), PIECE)
-        return remote(f.at[b, other], f.at[b, other], fw_send.at[b, j], fw_recv.at[b, j], sibling())
+    def piece_at(gr, j):
+        return pl.ds(pl.multiple_of(j * PIECES[gr], 16), PIECES[gr])
+
+    def f_at(gr, c, j):
+        return pl.ds(pl.multiple_of(BASES[gr] + (c * 16 + j) * PIECES[gr], 16), PIECES[gr])
+
+    def core_copy(gr):
+        rows = 16 * PIECES[gr]
+        there = pl.ds(pl.multiple_of((1 - core) * rows, 16), rows)
+        return remote(gs[gr].at[there], r0s[gr], core_send.at[gr], core_recv.at[gr], sibling())
+
+    def xy_copy(gr, j, slot):
+        return remote(
+            hhs[gr].at[piece_at(gr, j)], rrs[gr].at[slot],
+            xy_send.at[gr, j], xy_recv.at[gr, slot], xy_dev(j),
+        )
+
+    def z_copy(gr, j, slot):
+        return remote(zs[gr].at[slot], zs[gr].at[slot], z_send.at[gr, j], z_recv.at[gr, slot], z_dev(j))
+
+    def ag_copy(gr, j, slot):
+        at = f_at(gr, core, slot)
+        return remote(f.at[at], f.at[at], ag_send.at[gr, j], ag_recv.at[gr, slot], xy_dev(j))
+
+    def fw_copy(gr, j, c):
+        at = f_at(gr, c, j)
+        return remote(f.at[at], f.at[at], fw_send.at[gr, j], fw_recv.at[gr, j], sibling())
 
     def xy_others(body):
         def step(k, carry):
@@ -410,118 +427,191 @@
             return carry
         lax.fori_loop(1, 8, step, 0)
 
-    def sum_0(b):
-        core_copy(b).start()
-
-    def sum_1(b):
-        core_copy(b).wait()
-        def step(j, carry):
-            own = g[b, pl.ds(pl.multiple_of(core * HALF + j * PIECE, 16), PIECE), :].astype(F32)
-            hh[b, piece_at(j), :] = (own + r0[b, piece_at(j), :].astype(F32)).astype(BF16)
-            return carry
-        lax.fori_loop(0, 16, step, 0)
-        xy_others(lambda j: xy_copy(b, j, me_xy).start())
-
-    def sum_2(b):
-        xy_others(lambda j: xy_copy(b, me_xy, j).wait_recv())
-        rr1[b, me_xy] = hh[b, piece_at(me_xy), :]
-        total = lax.fori_loop(
-            0, 16, lambda j, a: a + rr1[b, j].astype(F32), jnp.zeros((PIECE, 128), F32)
-        )
-        z[b, 0:PIECE, :] = total.astype(BF16)
-        z[b, PIECE:, :] = jnp.zeros((16, 128), BF16)
-        z_others(lambda j: z_copy(b, j, zi).start())
-
-    def sum_3(b):
-        z_others(lambda j: z_copy(b, zi, j).wait_recv())
-        rr2[b, zi] = z[b, tile_at(zi), :]
-        total = jnp.zeros((16, 128), F32)
-        for j in range(8):
-            total = total + rr2[b, j].astype(F32)
-        zg[b, tile_at(zi), :] = total.astype(BF16)
-        z_others(lambda j: zg_copy(b, j, zi).start())
-
-    def sum_4(b):
-        z_others(lambda j: zg_copy(b, zi, j).wait_recv())
-        f[b, f_at(me_xy), :] = zg[b, 0:PIECE, :]
-        xy_others(lambda j: ag_copy(b, j, me_xy).start())
-        fw_copy(b, me_xy).start()
-
-    def sum_5(b):
+    def sum_0(gr):
+        core_copy(gr).start()
+
+    def sum_1(gr):
+        core_copy(gr).wait()
+
+        def add(j):
+            own = gs[gr][pl.ds(pl.multiple_of((core * 16 + j) * PIECES[gr], 16), PIECES[gr]), :]
+            there = r0s[gr][piece_at(gr, j), :]
+            hhs[gr][piece_at(gr, j), :] = (own.astype(F32) + there.astype(F32)).astype(BF16)
+
+        def add_and_send(j):
+            add(j)
+            xy_copy(gr, j, me_xy).start()
+
+        xy_others(add_and_send)
+        add(me_xy)
+
+    def sum_2(gr):
+        def step(k, total):
+            j = lax.rem(me_xy + k, 16)
+            xy_copy(gr, me_xy, j).wait_recv()
+            return total + rrs[gr][j].astype(F32)
+
+        own = hhs[gr][piece_at(gr, me_xy), :].astype(F32)
+        zs[gr][zi] = lax.fori_loop(1, 16, step, own).astype(BF16)
+        z_others(lambda j: z_copy(gr, j, zi).start())
+
+    def sum_3(gr):
+        z_others(lambda j: z_copy(gr, zi, j).wait_recv())
+        total = zs[gr][0].astype(F32)
+        for j in range(1, 8):
+            total = total + zs[gr][j].astype(F32)
+        f[f_at(gr, core, me_xy), :] = total.astype(BF16)
+        xy_others(lambda j: ag_copy(gr, j, me_xy).start())
+        fw_copy(gr, me_xy, core).start()
+
+    def sum_4(gr):
         def forward(j):
-            ag_copy(b, me_xy, j).wait_recv()
-            fw_copy(b, j).start()
+            ag_copy(gr, me_xy, j).wait_recv()
+            fw_copy(gr, j, core).start()
         xy_others(forward)
 
-    def sum_6(b):
+    def sum_5(gr):
         def arrived(j, carry):
-            fw_arrived(b, j).wait_recv()
-            fw_copy(b, j).wait_send()
+            fw_copy(gr, j, 1 - core).wait_recv()
+            fw_copy(gr, j, core).wait_send()
             return carry
         lax.fori_loop(0, 16, arrived, 0)
+
+    def sum_sent(gr):
         def sent(j):
-            xy_copy(b, j, me_xy).wait_send()
-            ag_copy(b, j, me_xy).wait_send()
+            xy_copy(gr, j, me_xy).wait_send()
+            ag_copy(gr, j, me_xy).wait_send()
         xy_others(sent)
-        def sent_z(j):
-            z_copy(b, j, zi).wait_send()
-            zg_copy(b, j, zi).wait_send()
-        z_others(sent_z)
-
+        z_others(lambda j: z_copy(gr, j, zi).wait_send())
+
+    def out_copy(gr):
+        at = pl.ds(BASES[gr], 32 * PIECES[gr])
+        return pltpu.make_async_copy(f.at[at], f_o.at[at], out_sem.at[gr])
+
+    def aside(w):
+        @pl.when(w == 1)
+        def _():
+            sum_1(1)
+
+        @pl.when(w == 3)
+        def _():
+            sum_2(0)
+
+    for gr in range(3):
+        used = (18, 12, 6)[gr] * D
+        gs[gr][used:, :] = jnp.zeros((32 * PIECES[gr] - used, 128), BF16)
     tile_to_windows(tok, cur)
     tile_to_windows(ct, cw)
+    prepare(0)
     pl.semaphore_wait(barrier, 29)
     halo_start(0, cw, 1)
-    block_forward(0, cur, nxt)
+    block_forward(0, cur, nxt, 1, 4)
     halo_start(1, nxt, 1)
-    halo_finish(1, nxt, cur, 1)
-    block_forward(1, cur, nxt)
-    halo_start(2, nxt, -1)
+    block_forward(0, cur, nxt, 0, 1)
+    prepare(1)
+    unpack_shift(nxt, halo_f, cur, 1, (3,))
+    block_forward(1, cur, out2, 3, 4)
+    halo_finish(1, nxt, cur, 1, (0, 1, 2))
+    block_forward(1, cur, out2, 0, 3)
+    halo_start(2, out2, -1)
     halo_finish(0, cw, cur, 1)
-    block_backward(1, cur, cw)
+    mlp_backward(1, cur, 0, 3)
+    attention_backward(1, 0, 3)
+    input_backward(1, cw, 0, 3)
     halo_start(3, cw, -1)
-    weight_terms(1)
+    mlp_backward(1, cur, 3, 4)
+    attention_backward(1, 3, 4)
+    input_backward(1, cw, 3, 4)
+    mlp_terms(1, 0, 6 * D)
+    attention_terms(1, 0, 0)
+    sum_0(0)
+    unpack_shift(cw, halo_f, nxt, -1, (0,))
+    mlp_backward(0, nxt, 0, 1)
+    sum_1(0)
+    halo_finish(3, cw, nxt, -1, (1, 2, 3))
+    mlp_backward(0, nxt, 1, 4)
+    mlp_terms(0, 1, 0)
     sum_0(1)
-    halo_finish(2, nxt, cur, -1)
-    windows_to_tile(cur, res_o)
-    halo_finish(3, cw, nxt, -1)
-    block_backward(0, nxt, cur)
-    weight_terms(0)
+    attention_backward(0, 0, 4, aside)
+    attention_terms(0, 2, 0)
+    sum_0(2)
+    input_backward(0, cur, 0, 4)
+    sum_1(2)
     windows_to_tile(cur, gt_o)
-    sum_0(0)
-    sum_1(1)
-    sum_1(0)
+    halo_finish(2, out2, nxt, -1)
+    windows_to_tile(nxt, res_o)
     sum_2(1)
-    sum_2(0)
+    sum_3(0)
+    sum_2(2)
     sum_3(1)
-    sum_3(0)
+    sum_4(0)
+    sum_3(2)
     sum_4(1)
-    sum_4(0)
-    sum_5(1)
-    sum_5(0)
-    sum_6(1)
-    sum_6(0)
-    out = pltpu.make_async_copy(f, f_o, out_sem)
-    out.start()
-    out.wait()
-
-
-def unpack_kernel(factor, f, res, gt, res_o, gt_o, *outs):
-    res_o[...] = res[...]
-    gt_o[...] = gt[...]
-    for b in range(2):
-        qkv, proj, up, down = outs[4 * b : 4 * b + 4]
-
-        def tile(i):
-            return f[b, i * D : i * D + D, :].astype(F32) * factor
-
-        for i in range(3):
-            two = jnp.concatenate([tile(2 * i), tile(2 * i + 1)], axis=1)
-            qkv[:, D * i : D * i + D] = two[:, 0:D]
-            proj[:, 64 * i : 64 * i + 64] = two[:, D:]
-        for i in range(6):
-            up[:, 128 * i : 128 * i + 128] = tile(6 + i)
-            down[128 * i : 128 * i + 128, :] = tile(12 + i).T
+    sum_4(2)
+    for gr in range(3):
+        sum_5(gr)
+        out_copy(gr).start()
+    for gr in range(3):
+        sum_sent(gr)
+        out_copy(gr).wait()
+
+
+def unpack_kernel(factor, f_in, res, gt, res_o, gt_o, *refs):
+    outs, f, held, sems = refs[:8], refs[8], refs[9:17], refs[17]
+    res_v, gt_v = refs[18], refs[19]
+    copies = []
+    fields = [
+        pltpu.make_async_copy(res, res_v, sems.at[0]),
+        pltpu.make_async_copy(gt, gt_v, sems.at[1]),
+    ]
+    parts = [
+        pltpu.make_async_copy(f_in.at[at], f.at[at], sems.at[2 + i])
+        for i, at in enumerate(
+            pl.ds(BASES[gr], 32 * PIECES[gr]) for gr in range(3)
+        )
+    ]
+    for copy in parts + fields:
+        copy.start()
+
+    def tile(gr, i):
+        at = BASES[gr] + i * D
+        return f[at : at + D, :].astype(F32) * factor
+
+    def attention_out(gr, i, qkv, proj):
+        for n in range(3):
+            two = jnp.concatenate([tile(gr, i + 2 * n), tile(gr, i + 2 * n + 1)], axis=1)
+            qkv[:, D * n : D * n + D] = two[:, 0:D]
+            proj[:, 64 * n : 64 * n + 64] = two[:, D:]
+
+    def mlp_out(gr, i, up, down):
+        for n in range(6):
+            up[:, 128 * n : 128 * n + 128] = tile(gr, i + n)
+            down[:, 128 * n : 128 * n + 128] = tile(gr, i + 6 + n)
+
+    def send(first, count):
+        for i in range(first, first + count):
+            copy = pltpu.make_async_copy(held[i], outs[i], sems.at[5 + i])
+            copy.start()
+            copies.append(copy)
+
+    parts[0].wait()
+    mlp_out(0, 6, held[6], held[7])
+    send(6, 2)
+    attention_out(0, 0, held[4], held[5])
+    send(4, 2)
+    for i, (held_f, out_f) in enumerate(((res_v, res_o), (gt_v, gt_o))):
+        fields[i].wait()
+        copy = pltpu.make_async_copy(held_f, out_f, sems.at[i])
+        copy.start()
+        copies.append(copy)
+    parts[1].wait()
+    mlp_out(1, 0, held[2], held[3])
+    send(2, 2)
+    parts[2].wait()
+    attention_out(2, 0, held[0], held[1])
+    send(0, 2)
+    for copy in copies:
+        copy.wait()
 
 
 def body(
@@ -552,6 +642,7 @@
         pltpu.VMEM((576, D), F32),
         pltpu.VMEM((576, D), F32),
         pltpu.VMEM((576, D), F32),
+        pltpu.VMEM((576, D), F32),
         pltpu.VMEM((HALO_ROWS, D), F32),
         pltpu.VMEM((HALO_ROWS, D), F32),
         pltpu.VMEM((4, HALO_ROWS, D), BF16),
@@ -565,26 +656,23 @@
         pltpu.VMEM((WIN, STACK), BF16),
         pltpu.VMEM((576, 768), BF16),
         pltpu.VMEM((D, 768), F32),
-        pltpu.VMEM((2, ROWS, 128), BF16),
-        pltpu.VMEM((2, HALF, 128), BF16),
-        pltpu.VMEM((2, HALF, 128), BF16),
-        pltpu.VMEM((2, 16, PIECE, 128), BF16),
-        pltpu.VMEM((2, 128, 128), BF16),
-        pltpu.VMEM((2, 8, 16, 128), BF16),
-        pltpu.VMEM((2, 128, 128), BF16),
-        pltpu.VMEM((2, ROWS, 128), BF16),
+        *[pltpu.VMEM((32 * r, 128), BF16) for r in PIECES],
+        *[pltpu.VMEM((16 * r, 128), BF16) for r in PIECES],
+        *[pltpu.VMEM((16 * r, 128), BF16) for r in PIECES],
+        *[pltpu.VMEM((16, r, 128), BF16) for r in PIECES],
+        *[pltpu.VMEM((8, r, 128), BF16) for r in PIECES],
+        pltpu.VMEM((ROWS, 128), BF16),
         dma(4, 3), dma(4, 3),
-        dma(2), dma(2),
-        dma(2, 16), dma(2, 16),
-        dma(2, 8), dma(2, 8),
-        dma(2, 8), dma(2, 8),
-        dma(2, 16), dma(2, 16),
-        dma(2, 16), dma(2, 16),
-        pltpu.SemaphoreType.DMA,
+        dma(3), dma(3),
+        dma(3, 16), dma(3, 16),
+        dma(3, 8), dma(3, 8),
+        dma(3, 16), dma(3, 16),
+        dma(3, 16), dma(3, 16),
+        dma(3),
     ]
     res, gt, f = pl.pallas_call(
         megakernel,
-        out_shape=(tile, tile, jax.ShapeDtypeStruct((2, ROWS, 128), BF16)),
+        out_shape=(tile, tile, jax.ShapeDtypeStruct((ROWS, 128), BF16)),
         in_specs=[vmem] * 16,
         out_specs=(vmem, vmem, pl.BlockSpec(memory_space=pl.ANY)),
         scratch_shapes=scratch,
@@ -593,24 +681,29 @@
         ),
     )(
         tokens.reshape(24, 24, D), cotangent.reshape(24, 24, D),
-        ga1, qkv1, proj1, gm1, up1, dn1, bias1.reshape(2, HEADS * WIN, WIN),
-        ga2, qkv2, proj2, gm2, up2, dn2, bias2.reshape(2, HEADS * WIN, WIN),
+        ga1, qkv1, proj1, gm1, up1, dn1.T, bias1.reshape(2, HEADS * WIN, WIN),
+        ga2, qkv2, proj2, gm2, up2, dn2.T, bias2.reshape(2, HEADS * WIN, WIN),
     )
     one = [
         jax.ShapeDtypeStruct((D, 3 * D), F32),
         jax.ShapeDtypeStruct((D, D), F32),
         jax.ShapeDtypeStruct((D, 4 * D), F32),
-        jax.ShapeDtypeStruct((4 * D, D), F32),
+        jax.ShapeDtypeStruct((D, 4 * D), F32),
     ]
-    outs = pl.pallas_call(
+    anywhere = pl.BlockSpec(memory_space=pl.ANY)
+    outs = list(pl.pallas_call(
         functools.partial(unpack_kernel, 1.0 / math.sqrt(256.0 * 576.0)),
         out_shape=[tile, tile] + one + one,
-        in_specs=[vmem] * 3,
-        out_specs=[vmem] * 10,
-        compiler_params=pltpu.CompilerParams(vmem_limit_bytes=48 * 1024 * 1024),
-    )(f, res, gt)
+        in_specs=[anywhere] * 3,
+        out_specs=[anywhere] * 10,
+        scratch_shapes=[pltpu.VMEM((ROWS, 128), BF16)]
+        + [pltpu.VMEM(s.shape, F32) for s in one + one]
+        + [dma(13), pltpu.VMEM(tile.shape, BF16), pltpu.VMEM(tile.shape, BF16)],
+        compiler_params=pltpu.CompilerParams(vmem_limit_bytes=60 * 1024 * 1024),
+    )(f, res, gt))
     shape = (2, 12, 24, D)
-    return (outs[0].reshape(shape), outs[1].reshape(shape)) + tuple(outs[2:])
+    terms = outs[2:5] + [outs[5].T] + outs[6:9] + [outs[9].T]
+    return (outs[0].reshape(shape), outs[1].reshape(shape)) + tuple(terms)
 
 
 def solution(mesh):

time: 104 us -> 80.3 us (0.77)
  Pallas kernels: 93.3 us -> 79.5 us
  local copies, waits for them, and re-layouts: 9.3 us -> 0 us
    pallas_call x1, Pallas kernels: 91.1 us -> 76 us  [body(): pl.pallas_call(megakernel, out_shape=(tile, tile, jax.ShapeDtypeStruct((R...]
    unnamed x10 -> x0, local copies, waits for them, and re-layouts: 9.3 us -> none
    pallas_call x1, Pallas kernels: 2.23 us -> 3.47 us  [body(): pl.pallas_call(functools.partial(unpack_kernel, 1.0 / math.sqrt(256.0 * 5...]
where the time goes in v1:
time: 80.3 us; the launch traced here: 80.2 us
  Pallas kernels  79.5 us (99%)
    pallas_call x1, Pallas kernels, body(): pl.pallas_call(megakernel, out_shape=(tile, tile, jax.ShapeDtypeStruct((R...  76 us
    pallas_call x1, Pallas kernels, body(): pl.pallas_call(functools.partial(unpack_kernel, 1.0 / math.sqrt(256.0 * 5...  3.47 us

profile of v1, /device:TPU:1, one launch (start us, length us, event | category | flops | bytes accessed | tf_op | source)
XLA Modules:
  0.0 80.2 jit_solution(9030800631684301014)
XLA Ops:
  0.6 76.0 %shard_map.231 = (bf16[24,24,192]{2,1,0:T(8,128)(2,1)}, bf16[24,24,192]{2,1,0:T(8,128)(2,1)}, bf16[7680,128]{1,0:T(8,128)(2,1)}) custom-call(bf16[24,24,192]{2,1,0:T(8,128)(2,1)} %bitcast.12, bf16[24,24,192]{2,1,0:T(8,128)(2,1)} %bitcast.13, f32[192]{0:T(256)} %ga1.1, bf16[192,576]{1,0:T(8,128)(2,1)} %qkv1.1, bf16[192,192]{1,0:T(8,128)(2,1)} %proj1.1, ...), custom_call_target="tpu_custom_call" | custom-call | tf_op jit(solution)/shard_map/pallas_call | solution.py:673
  76.7 3.5 %shard_map.232 = (bf16[24,24,192]{2,1,0:T(8,128)(2,1)}, bf16[24,24,192]{2,1,0:T(8,128)(2,1)}, f32[192,576]{1,0:T(8,128)}, f32[192,192]{1,0:T(8,128)}, f32[192,76...) custom-call(bf16[7680,128]{1,0:T(8,128)(2,1)} %get-tuple-element.23., ...), custom_call_target="tpu_custom_call" | custom-call | tf_op jit(solution)/shard_map/pallas_call | solution.py:694

commit v2 on v1

--- a/solution.py
+++ b/solution.py
@@ -17,9 +17,10 @@
 STACK = 896
 SCALE = 32 ** -0.5
 CHUNKS = ((0, 256), (256, 512), (512, 768), (768, 896))
-PIECES = (112, 80, 48)
-BASES = (0, 32 * 112, 32 * 192)
-ROWS = 32 * 240
+PIECES = (80, 48, 80, 48)
+BASES = (0, 32 * 80, 32 * 128, 32 * 208)
+ROWS = 32 * 256
+GROUPS = 4
 MESH = pl.DeviceIdType.MESH
 
 
@@ -43,17 +44,23 @@
     return pl.ds(pl.multiple_of(w * WIN, 16), WIN)
 
 
-def normalise(x):
-    mean = jnp.mean(x, axis=-1, keepdims=True)
+def lane_mean(x):
+    return dot_nn(x, jnp.ones((D, D), BF16)) * (1.0 / D)
+
+
+def normalise(x, exact):
+    high = x.astype(BF16)
+    mean = lane_mean(high)
+    if not exact:
+        mean = mean + lane_mean((x - high.astype(F32)).astype(BF16))
     centred = x - mean
-    var = jnp.mean(centred * centred, axis=-1, keepdims=True)
-    r = lax.rsqrt(var + 1e-05)
+    r = lax.rsqrt(lane_mean((centred * centred).astype(BF16)) + 1e-05)
     return centred * r, r
 
 
 def normalise_back(dy, xhat, r):
-    m1 = jnp.mean(dy, axis=-1, keepdims=True)
-    m2 = jnp.mean(dy * xhat, axis=-1, keepdims=True)
+    m1 = lane_mean(dy.astype(BF16))
+    m2 = lane_mean((dy * xhat).astype(BF16))
     return r * (dy - m1 - xhat * m2)
 
 
@@ -71,6 +78,17 @@
     lane = lax.broadcasted_iota(jnp.int32, (1, D), 1)
     inside = (lane >= 32 * h) & (lane < 32 * h + 32)
     return jnp.where(inside, 1.0, 0.0).astype(F32).astype(dtype)
+
+
+def own_lanes(o):
+    lane = lax.broadcasted_iota(jnp.int32, (1, 128), 1)
+    left = o[3 * WIN : 4 * WIN, 0:128]
+    for h in (2, 1, 0):
+        left = jnp.where(lane < 32 * h + 32, o[WIN * h : WIN * h + WIN, 0:128], left)
+    right = jnp.where(
+        lane[:, 0:64] < 32, o[4 * WIN : 5 * WIN, 128:D], o[5 * WIN : 6 * WIN, 128:D]
+    )
+    return jnp.concatenate([left, right], axis=1)
 
 
 def tile_to_windows(src, dst):
@@ -141,19 +159,27 @@
 
 
 def megakernel(
-    tok, ct,
-    ga1, qkv1, proj1, gm1, up1, dn1, bias1,
-    ga2, qkv2, proj2, gm2, up2, dn2, bias2,
+    ga1, gm1, ga2, gm2, tok, ct, qkv1, proj1, up1, dn1, bias1, qkv2, proj2, up2, dn2, bias2,
     res_o, gt_o, f_o,
-    wp, bt, xhat1, r1, normed, proj_all, qm, pt, att, xhat2, r2, second, hidden, gp,
-    cur, nxt, out2, cw, pack, halo_f, halo_out, halo_in,
-    dtot, du, dres, dres_b, datt, dom, dst_, dqkv, w6,
-    g_0, g_1, g_2, r_0, r_1, r_2, h_0, h_1, h_2, rr_0, rr_1, rr_2, z_0, z_1, z_2, f,
-    halo_send, halo_recv, core_send, core_recv, xy_send, xy_recv, z_send, z_recv,
-    ag_send, ag_recv, fw_send, fw_recv, out_sem,
+    wp, bt, alive, xhat1, r1, normed, proj_all, qm, pt, att, xhat2, r2, second, hidden, gp,
+    res_v, gt_v, f, cur, nxt, out2, cw, pack, halo_f, halo_out, halo_in,
+    dtot, du, dres, dres_b, datt, dom, dst_, dqkv, w6, *refs
 ):
-    gs, r0s, hhs = (g_0, g_1, g_2), (r_0, r_1, r_2), (h_0, h_1, h_2)
-    rrs, zs = (rr_0, rr_1, rr_2), (z_0, z_1, z_2)
+    gs, r0s, hhs, rrs, zs = (refs[GROUPS * i : GROUPS * i + GROUPS] for i in range(5))
+    held, sems = refs[5 * GROUPS : 5 * GROUPS + 12], refs[5 * GROUPS + 12 :]
+    (
+        halo_send, halo_recv, core_send, core_recv, xy_send, xy_recv, z_send, z_recv,
+        ag_send, ag_recv, fw_send, fw_recv, out_sem, in_sem,
+    ) = sems
+    loads = [
+        pltpu.make_async_copy(there, here, in_sem.at[i])
+        for i, (there, here) in enumerate(
+            zip((tok, ct, qkv1, proj1, up1, dn1, bias1, qkv2, proj2, up2, dn2, bias2), held)
+        )
+    ]
+    for i in (0, 2, 6, 1, 3, 4, 5, 7, 11, 8, 9, 10):
+        loads[i].start()
+    tok, ct, qkv1, proj1, up1, dn1, bias1, qkv2, proj2, up2, dn2, bias2 = held
     lon = lax.axis_index("lon")
     lat = lax.axis_index("lat")
     core = lax.rem(lon, 2)
@@ -227,9 +253,6 @@
         (ga2, qkv2, proj2, gm2, up2, dn2, bias2),
     )
 
-    def live(b, w):
-        return live_column(starts[b] + 6 * (w // 2), limit)
-
     def prepare(b):
         ga, wqkv, wproj, gm, wup, wdn, bias = weights[b]
         wp[b] = jnp.zeros((D, 768), BF16)
@@ -240,7 +263,10 @@
         cols_i = lax.broadcasted_iota(jnp.int32, (WIN, WIN), 1)
         eye = jnp.where(rows_i == cols_i, 1.0, 0.0).astype(F32).astype(BF16)
         for wr in range(2):
-            penalty = (live_column(starts[b] + 6 * wr, limit) - 1.0) * 30000.0
+            here = live_column(starts[b] + 6 * wr, limit)
+            penalty = (here - 1.0) * 30000.0
+            for wc in range(2):
+                alive[b, (2 * wr + wc) * WIN : (2 * wr + wc + 1) * WIN, :] = here
             bt[wr, :, 0:864] = dot_nt(eye, bias[wr]) + penalty
             bt[wr, :, 864:] = jnp.zeros((WIN, STACK - 864), F32)
 
@@ -249,16 +275,16 @@
         gain_a = ga[...].reshape(1, D)
         gain_m = gm[...].reshape(1, D)
 
-        def f_qkv(w):
-            rows = win_rows(w)
-            xh, r = normalise(x_in[rows, :])
-            xhat1[b, rows, :] = xh
-            r1[b, rows, :] = r
-            nb = (xh * gain_a).astype(BF16)
-            normed[b, rows, :] = nb
-            proj_all[b, rows, :] = dot_nn(nb, wp[b]).astype(BF16)
-
-        stage("f_qkv", lambda: pl.loop(lo, hi)(f_qkv))
+        span = slice(lo * WIN, hi * WIN)
+
+        def f_qkv():
+            xh, r = normalise(x_in[span, :], True)
+            xhat1[b, span, :] = xh
+            r1[b, span, :] = r
+            normed[b, span, :] = (xh * gain_a).astype(BF16)
+            proj_all[b, span, :] = dot_nn(normed[b, span, :], wp[b]).astype(BF16)
+
+        stage("f_qkv", f_qkv)
 
         def f_att(w):
             rows = win_rows(w)
@@ -275,55 +301,53 @@
                 total = jnp.sum(e, axis=0, keepdims=True)
                 pt[b, w, :, c0:c1] = (e * (1.0 / total)).astype(BF16)
             o = dot_tn(pt[b, w], v)
-            a = jnp.zeros((WIN, D), F32)
-            for h in range(HEADS):
-                a = a + o[WIN * h : WIN * h + WIN, :] * head_mask(h, F32)
+            a = own_lanes(o)
             att[b, rows, :] = a.astype(BF16)
 
-        stage("f_att", lambda: pl.loop(lo, hi)(f_att))
-
-        def f_mlp(w):
-            rows = win_rows(w)
-            resid = x_in[rows, :] + dot_nn(att[b, rows, :], wproj[...])
-            xh, r = normalise(resid)
-            xhat2[b, rows, :] = xh
-            r2[b, rows, :] = r
-            sb = (xh * gain_m).astype(BF16)
-            second[b, rows, :] = sb
-            u = dot_nn(sb, wup[...])
+        stage("f_att", lambda: [f_att(w) for w in range(lo, hi)])
+
+        def f_mlp():
+            resid = x_in[span, :] + dot_nn(att[b, span, :], wproj[...])
+            x_out[span, :] = resid
+            xh, r = normalise(resid, False)
+            xhat2[b, span, :] = xh
+            r2[b, span, :] = r
+            second[b, span, :] = (xh * gain_m).astype(BF16)
             c = math.sqrt(2.0 / math.pi)
-            u2 = u * u
-            t = jnp.tanh(u * (c + (c * 0.044715) * u2))
-            half = 0.5 + 0.5 * t
-            hb = (u * half).astype(BF16)
-            hidden[b, rows, :] = hb
-            slope = half + u * (0.5 - 0.5 * t * t) * (c + (3 * c * 0.044715) * u2)
-            gp[b, rows, :] = slope.astype(BF16)
-            out = (resid + dot_nt(hb, wdn[...])) * live(b, w)
-            x_out[rows, :] = out.astype(BF16).astype(F32)
-
-        stage("f_mlp", lambda: pl.loop(lo, hi)(f_mlp))
+            for n in range(3):
+                at = slice(256 * n, 256 * n + 256)
+                u = dot_nn(second[b, span, :], wup[:, at])
+                u2 = u * u
+                t = jnp.tanh(u * (c + (c * 0.044715) * u2))
+                half = 0.5 + 0.5 * t
+                hidden[b, span, at] = (u * half).astype(BF16)
+                slope = half + u * (half * (1.0 - half)) * (2 * c + (6 * c * 0.044715) * u2)
+                gp[b, span, at] = slope.astype(BF16)
+            out = (x_out[span, :] + dot_nt(hidden[b, span, :], wdn[...])) * alive[b, span, :]
+            x_out[span, :] = out.astype(BF16).astype(F32)
+
+        stage("f_mlp", f_mlp)
 
     def mlp_backward(b, d_out, lo, hi):
         ga, wqkv, wproj, gm, wup, wdn, bias = weights[b]
         gain_m = gm[...].reshape(1, D)
 
-        def b_mlp(w):
-            rows = win_rows(w)
-            dt = d_out[rows, :] * live(b, w)
-            dtb = dt.astype(BF16)
-            dtot[rows, :] = dtb
-            dh = dot_nn(dtb, wdn[...]).astype(BF16).astype(F32)
-            dub = (dh * gp[b, rows, :].astype(F32)).astype(BF16)
-            du[rows, :] = dub
-            dy = dot_nt(dub, wup[...]).astype(BF16).astype(F32) * gain_m
-            dr = dt + normalise_back(dy, xhat2[b, rows, :], r2[b, rows, :])
-            dres[rows, :] = dr
-            drb = dr.astype(BF16)
-            dres_b[rows, :] = drb
-            datt[rows, :] = dot_nt(drb, wproj[...]).astype(BF16)
-
-        stage("b_mlp", lambda: pl.loop(lo, hi)(b_mlp))
+        span = slice(lo * WIN, hi * WIN)
+
+        def b_mlp():
+            dtb = (d_out[span, :] * alive[b, span, :]).astype(BF16)
+            dtot[span, :] = dtb
+            for n in range(3):
+                at = slice(256 * n, 256 * n + 256)
+                dh = dot_nn(dtot[span, :], wdn[:, at]).astype(BF16).astype(F32)
+                du[span, at] = (dh * gp[b, span, at].astype(F32)).astype(BF16)
+            dy = dot_nt(du[span, :], wup[...]).astype(BF16).astype(F32) * gain_m
+            dr = dtot[span, :].astype(F32) + normalise_back(dy, xhat2[b, span, :], r2[b, span, :])
+            dres[span, :] = dr
+            dres_b[span, :] = dr.astype(BF16)
+            datt[span, :] = dot_nt(dres_b[span, :], wproj[...]).astype(BF16)
+
+        stage("b_mlp", b_mlp)
 
     def attention_backward(b, lo, hi, between=None):
         def b_att(w):
@@ -332,20 +356,18 @@
             v = proj_all[b, rows, 512 : 512 + D]
             do = datt[rows, :]
             for h in range(HEADS):
-                dom[WIN * h : WIN * h + WIN, :] = do * head_mask(h, BF16)
-            dom[864:, :] = jnp.zeros((STACK - 864, D), BF16)
+                dom[w, WIN * h : WIN * h + WIN, :] = do * head_mask(h, BF16)
+            dom[w, 864:, :] = jnp.zeros((STACK - 864, D), BF16)
             for c0, c1 in CHUNKS:
-                dp = dot_nt(v, dom[c0:c1, :]).astype(BF16).astype(F32)
+                dp = dot_nt(v, dom[w, c0:c1, :]).astype(BF16).astype(F32)
                 p = pt[b, w, :, c0:c1].astype(F32)
                 delta = jnp.sum(p * dp, axis=0, keepdims=True)
-                dst_[:, c0:c1] = (p * (dp - delta)).astype(BF16)
+                dst_[w, :, c0:c1] = (p * (dp - delta)).astype(BF16)
             zeros = jnp.zeros((WIN, 64), BF16)
-            dqkv[rows, 512 : 512 + D] = dot_nn(pt[b, w], dom[...]).astype(BF16)
-            dqkv[rows, 256 : 256 + D] = (dot_nn(dst_[...], qm[b, w]) * SCALE).astype(BF16)
-            o = dot_tn(dst_[...], k)
-            a = jnp.zeros((WIN, D), F32)
-            for h in range(HEADS):
-                a = a + o[WIN * h : WIN * h + WIN, :] * head_mask(h, F32)
+            dqkv[rows, 512 : 512 + D] = dot_nn(pt[b, w], dom[w]).astype(BF16)
+            dqkv[rows, 256 : 256 + D] = (dot_nn(dst_[w], qm[b, w]) * SCALE).astype(BF16)
+            o = dot_tn(dst_[w], k)
+            a = own_lanes(o)
             dqkv[rows, 0:D] = (a * SCALE).astype(BF16)
             for i in range(3):
                 dqkv[rows, 256 * i + D : 256 * i + 256] = zeros
@@ -353,18 +375,19 @@
             if between is not None:
                 between(w)
 
-        stage("b_att", lambda: pl.loop(lo, hi)(b_att))
+        stage("b_att", lambda: [b_att(w) for w in range(lo, hi)])
 
     def input_backward(b, d_in, lo, hi):
         gain_a = weights[b][0][...].reshape(1, D)
 
-        def b_qkv(w):
-            rows = win_rows(w)
-            dy = dot_nt(dqkv[rows, :], wp[b]).astype(BF16).astype(F32) * gain_a
-            dx = dres[rows, :] + normalise_back(dy, xhat1[b, rows, :], r1[b, rows, :])
-            d_in[rows, :] = dx.astype(BF16).astype(F32)
-
-        stage("b_qkv", lambda: pl.loop(lo, hi)(b_qkv))
+        span = slice(lo * WIN, hi * WIN)
+
+        def b_qkv():
+            dy = dot_nt(dqkv[span, :], wp[b]).astype(BF16).astype(F32) * gain_a
+            dx = dres[span, :] + normalise_back(dy, xhat1[b, span, :], r1[b, span, :])
+            d_in[span, :] = dx.astype(BF16).astype(F32)
+
+        stage("b_qkv", b_qkv)
 
     def put(gr, at, matrix):
         for i in range(6):
@@ -489,71 +512,91 @@
         return pltpu.make_async_copy(f.at[at], f_o.at[at], out_sem.at[gr])
 
     def aside(w):
-        @pl.when(w == 1)
-        def _():
-            sum_1(1)
-
-        @pl.when(w == 3)
-        def _():
-            sum_2(0)
-
-    for gr in range(3):
-        used = (18, 12, 6)[gr] * D
+        if w == 1:
+            sum_1(2)
+
+    def field_copy(i):
+        return pltpu.make_async_copy((res_v, gt_v)[i], (res_o, gt_o)[i], out_sem.at[GROUPS + i])
+
+    for gr in range(GROUPS):
+        used = (12, 6)[gr % 2] * D
         gs[gr][used:, :] = jnp.zeros((32 * PIECES[gr] - used, 128), BF16)
+    loads[0].wait()
     tile_to_windows(tok, cur)
+    loads[2].wait()
+    loads[6].wait()
+    stage("prepare", lambda: prepare(0))
+    loads[1].wait()
     tile_to_windows(ct, cw)
-    prepare(0)
     pl.semaphore_wait(barrier, 29)
     halo_start(0, cw, 1)
+    for i in (3, 4, 5):
+        loads[i].wait()
     block_forward(0, cur, nxt, 1, 4)
     halo_start(1, nxt, 1)
     block_forward(0, cur, nxt, 0, 1)
-    prepare(1)
+    for i in (7, 8, 9, 10, 11):
+        loads[i].wait()
+    stage("prepare", lambda: prepare(1))
     unpack_shift(nxt, halo_f, cur, 1, (3,))
     block_forward(1, cur, out2, 3, 4)
     halo_finish(1, nxt, cur, 1, (0, 1, 2))
     block_forward(1, cur, out2, 0, 3)
     halo_start(2, out2, -1)
     halo_finish(0, cw, cur, 1)
-    mlp_backward(1, cur, 0, 3)
+    mlp_backward(1, cur, 0, 4)
+    stage("mlp_terms", lambda: mlp_terms(1, 0, 0))
+    sum_0(0)
     attention_backward(1, 0, 3)
     input_backward(1, cw, 0, 3)
     halo_start(3, cw, -1)
-    mlp_backward(1, cur, 3, 4)
+    sum_1(0)
     attention_backward(1, 3, 4)
     input_backward(1, cw, 3, 4)
-    mlp_terms(1, 0, 6 * D)
-    attention_terms(1, 0, 0)
-    sum_0(0)
+    stage("attention_terms", lambda: attention_terms(1, 1, 0))
+    sum_0(1)
     unpack_shift(cw, halo_f, nxt, -1, (0,))
     mlp_backward(0, nxt, 0, 1)
-    sum_1(0)
+    sum_1(1)
     halo_finish(3, cw, nxt, -1, (1, 2, 3))
     mlp_backward(0, nxt, 1, 4)
-    mlp_terms(0, 1, 0)
-    sum_0(1)
+    stage("mlp_terms", lambda: mlp_terms(0, 2, 0))
+    sum_0(2)
+    sum_2(0)
     attention_backward(0, 0, 4, aside)
-    attention_terms(0, 2, 0)
-    sum_0(2)
+    stage("attention_terms", lambda: attention_terms(0, 3, 0))
+    sum_0(3)
     input_backward(0, cur, 0, 4)
-    sum_1(2)
-    windows_to_tile(cur, gt_o)
+    sum_1(3)
+    windows_to_tile(cur, gt_v)
+    field_copy(1).start()
+    sum_2(1)
     halo_finish(2, out2, nxt, -1)
-    windows_to_tile(nxt, res_o)
-    sum_2(1)
+    windows_to_tile(nxt, res_v)
+    field_copy(0).start()
     sum_3(0)
     sum_2(2)
     sum_3(1)
+    sum_2(3)
     sum_4(0)
     sum_3(2)
     sum_4(1)
+    sum_3(3)
+    sum_5(0)
+    out_copy(0).start()
     sum_4(2)
-    for gr in range(3):
-        sum_5(gr)
-        out_copy(gr).start()
-    for gr in range(3):
+    sum_5(1)
+    out_copy(1).start()
+    sum_4(3)
+    sum_5(2)
+    out_copy(2).start()
+    sum_5(3)
+    out_copy(3).start()
+    for gr in range(GROUPS):
         sum_sent(gr)
         out_copy(gr).wait()
+    field_copy(0).wait()
+    field_copy(1).wait()
 
 
 def unpack_kernel(factor, f_in, res, gt, res_o, gt_o, *refs):
@@ -564,12 +607,10 @@
         pltpu.make_async_copy(res, res_v, sems.at[0]),
         pltpu.make_async_copy(gt, gt_v, sems.at[1]),
     ]
-    parts = [
-        pltpu.make_async_copy(f_in.at[at], f.at[at], sems.at[2 + i])
-        for i, at in enumerate(
-            pl.ds(BASES[gr], 32 * PIECES[gr]) for gr in range(3)
-        )
-    ]
+    parts = []
+    for gr in range(GROUPS):
+        at = pl.ds(BASES[gr], 32 * PIECES[gr])
+        parts.append(pltpu.make_async_copy(f_in.at[at], f.at[at], sems.at[2 + gr]))
     for copy in parts + fields:
         copy.start()
 
@@ -590,25 +631,26 @@
 
     def send(first, count):
         for i in range(first, first + count):
-            copy = pltpu.make_async_copy(held[i], outs[i], sems.at[5 + i])
+            copy = pltpu.make_async_copy(held[i], outs[i], sems.at[2 + GROUPS + i])
             copy.start()
             copies.append(copy)
 
     parts[0].wait()
-    mlp_out(0, 6, held[6], held[7])
+    mlp_out(0, 0, held[6], held[7])
     send(6, 2)
-    attention_out(0, 0, held[4], held[5])
-    send(4, 2)
     for i, (held_f, out_f) in enumerate(((res_v, res_o), (gt_v, gt_o))):
         fields[i].wait()
         copy = pltpu.make_async_copy(held_f, out_f, sems.at[i])
         copy.start()
         copies.append(copy)
     parts[1].wait()
-    mlp_out(1, 0, held[2], held[3])
+    attention_out(1, 0, held[4], held[5])
+    send(4, 2)
+    parts[2].wait()
+    mlp_out(2, 0, held[2], held[3])
     send(2, 2)
-    parts[2].wait()
-    attention_out(2, 0, held[0], held[1])
+    parts[3].wait()
+    attention_out(3, 0, held[0], held[1])
     send(0, 2)
     for copy in copies:
         copy.wait()
@@ -624,21 +666,31 @@
     def dma(*shape):
         return pltpu.SemaphoreType.DMA(shape)
 
+    big = (
+        tokens.reshape(24, 24, D), cotangent.reshape(24, 24, D),
+        qkv1, proj1, up1, dn1.T, bias1.reshape(2, HEADS * WIN, WIN),
+        qkv2, proj2, up2, dn2.T, bias2.reshape(2, HEADS * WIN, WIN),
+    )
+    anywhere = pl.BlockSpec(memory_space=pl.ANY)
     scratch = [
         pltpu.VMEM((2, D, 768), BF16),
         pltpu.VMEM((2, WIN, STACK), F32),
+        pltpu.VMEM((2, 576, 1), F32),
         pltpu.VMEM((2, 576, D), F32),
-        pltpu.VMEM((2, 576, 1), F32),
+        pltpu.VMEM((2, 576, D), F32),
         pltpu.VMEM((2, 576, D), BF16),
         pltpu.VMEM((2, 576, 768), BF16),
         pltpu.VMEM((2, 4, STACK, D), BF16),
         pltpu.VMEM((2, 4, WIN, STACK), BF16),
         pltpu.VMEM((2, 576, D), BF16),
         pltpu.VMEM((2, 576, D), F32),
-        pltpu.VMEM((2, 576, 1), F32),
+        pltpu.VMEM((2, 576, D), F32),
         pltpu.VMEM((2, 576, D), BF16),
         pltpu.VMEM((2, 576, 768), BF16),
         pltpu.VMEM((2, 576, 768), BF16),
+        pltpu.VMEM((24, 24, D), BF16),
+        pltpu.VMEM((24, 24, D), BF16),
+        pltpu.VMEM((ROWS, 128), BF16),
         pltpu.VMEM((576, D), F32),
         pltpu.VMEM((576, D), F32),
         pltpu.VMEM((576, D), F32),
@@ -652,8 +704,8 @@
         pltpu.VMEM((576, D), F32),
         pltpu.VMEM((576, D), BF16),
         pltpu.VMEM((576, D), BF16),
-        pltpu.VMEM((STACK, D), BF16),
-        pltpu.VMEM((WIN, STACK), BF16),
+        pltpu.VMEM((4, STACK, D), BF16),
+        pltpu.VMEM((4, WIN, STACK), BF16),
         pltpu.VMEM((576, 768), BF16),
         pltpu.VMEM((D, 768), F32),
         *[pltpu.VMEM((32 * r, 128), BF16) for r in PIECES],
@@ -661,28 +713,26 @@
         *[pltpu.VMEM((16 * r, 128), BF16) for r in PIECES],
         *[pltpu.VMEM((16, r, 128), BF16) for r in PIECES],
         *[pltpu.VMEM((8, r, 128), BF16) for r in PIECES],
-        pltpu.VMEM((ROWS, 128), BF16),
+        *[pltpu.VMEM(a.shape, BF16) for a in big],
         dma(4, 3), dma(4, 3),
-        dma(3), dma(3),
-        dma(3, 16), dma(3, 16),
-        dma(3, 8), dma(3, 8),
-        dma(3, 16), dma(3, 16),
-        dma(3, 16), dma(3, 16),
-        dma(3),
+        dma(GROUPS), dma(GROUPS),
+        dma(GROUPS, 16), dma(GROUPS, 16),
+        dma(GROUPS, 8), dma(GROUPS, 8),
+        dma(GROUPS, 16), dma(GROUPS, 16),
+        dma(GROUPS, 16), dma(GROUPS, 16),
+        dma(GROUPS + 2), dma(12),
     ]
     res, gt, f = pl.pallas_call(
         megakernel,
         out_shape=(tile, tile, jax.ShapeDtypeStruct((ROWS, 128), BF16)),
-        in_specs=[vmem] * 16,
-        out_specs=(vmem, vmem, pl.BlockSpec(memory_space=pl.ANY)),
+        in_specs=[vmem] * 4 + [anywhere] * 12,
+        out_specs=(anywhere,) * 3,
         scratch_shapes=scratch,
         compiler_params=pltpu.CompilerParams(
-            collective_id=0, has_side_effects=True, vmem_limit_bytes=56 * 1024 * 1024
+            collective_id=0, has_side_effects=True, vmem_limit_bytes=60 * 1024 * 1024
         ),
     )(
-        tokens.reshape(24, 24, D), cotangent.reshape(24, 24, D),
-        ga1, qkv1, proj1, gm1, up1, dn1.T, bias1.reshape(2, HEADS * WIN, WIN),
-        ga2, qkv2, proj2, gm2, up2, dn2.T, bias2.reshape(2, HEADS * WIN, WIN),
+        ga1, gm1, ga2, gm2, *big
     )
     one = [
         jax.ShapeDtypeStruct((D, 3 * D), F32),
@@ -690,7 +740,6 @@
         jax.ShapeDtypeStruct((D, 4 * D), F32),
         jax.ShapeDtypeStruct((D, 4 * D), F32),
     ]
-    anywhere = pl.BlockSpec(memory_space=pl.ANY)
     outs = list(pl.pallas_call(
         functools.partial(unpack_kernel, 1.0 / math.sqrt(256.0 * 576.0)),
         out_shape=[tile, tile] + one + one,
@@ -698,7 +747,7 @@
         out_specs=[anywhere] * 10,
         scratch_shapes=[pltpu.VMEM((ROWS, 128), BF16)]
         + [pltpu.VMEM(s.shape, F32) for s in one + one]
-        + [dma(13), pltpu.VMEM(tile.shape, BF16), pltpu.VMEM(tile.shape, BF16)],
+        + [dma(10 + GROUPS), pltpu.VMEM(tile.shape, BF16), pltpu.VMEM(tile.shape, BF16)],
         compiler_params=pltpu.CompilerParams(vmem_limit_bytes=60 * 1024 * 1024),
     )(f, res, gt))
     shape = (2, 12, 24, D)

time: 80.3 us -> 70.6 us (0.88)
  Pallas kernels: 79.5 us -> 69.6 us
    pallas_call x1, Pallas kernels: 76 us -> 66.2 us  [body(): pl.pallas_call(megakernel, out_shape=(tile, tile, jax.ShapeDtypeStruct((R...]
where the time goes in v2:
time: 70.6 us; the launch traced here: 70.4 us
  Pallas kernels  69.6 us (99%)
  between operations  0.82 us (1%)
    pallas_call x1, Pallas kernels, body(): pl.pallas_call(megakernel, out_shape=(tile, tile, jax.ShapeDtypeStruct((R...  66.2 us
    pallas_call x1, Pallas kernels, body(): pl.pallas_call(functools.partial(unpack_kernel, 1.0 / math.sqrt(256.0 * 5...  3.4 us

profile of v2, /device:TPU:1, one launch (start us, length us, event | category | flops | bytes accessed | tf_op | source)
XLA Modules:
  0.0 70.4 jit_solution(2830510600169197373)
XLA Ops:
  0.6 66.2 %shard_map.231 = (bf16[24,24,192]{2,1,0:T(8,128)(2,1)}, bf16[24,24,192]{2,1,0:T(8,128)(2,1)}, bf16[8192,128]{1,0:T(8,128)(2,1)}) custom-call(f32[192]{0:T(256)} %ga1.1, f32[192]{0:T(256)} %gm1.1, f32[192]{0:T(256)} %ga2.1, f32[192]{0:T(256)} %gm2.1, bf16[24,24,192]{2,1,0:T(8,128)(2,1)} %bitcast.12, bf16[24,24,192]{2,1,0:T(8,128)(2,1)} %bitcast.13, ...), custom_call_target="tpu_custom_call" | custom-call | tf_op jit(solution)/shard_map/pallas_call | solution.py:725
  66.9 3.4 %shard_map.232 = (bf16[24,24,192]{2,1,0:T(8,128)(2,1)}, bf16[24,24,192]{2,1,0:T(8,128)(2,1)}, f32[192,576]{1,0:T(8,128)}, f32[192,192]{1,0:T(8,128)}, f32[192,76...) custom-call(bf16[8192,128]{1,0:T(8,128)(2,1)} %get-tuple-element.23., ...), custom_call_target="tpu_custom_call" | custom-call | tf_op jit(solution)/shard_map/pallas_call | solution.py:743

commit v3 on v2

--- a/solution.py
+++ b/solution.py
@@ -17,9 +17,9 @@
 STACK = 896
 SCALE = 32 ** -0.5
 CHUNKS = ((0, 256), (256, 512), (512, 768), (768, 896))
-PIECES = (80, 48, 80, 48)
-BASES = (0, 32 * 80, 32 * 128, 32 * 208)
-ROWS = 32 * 256
+PIECES = (80, 32, 80, 32)
+BASES = (0, 32 * 80, 32 * 112, 32 * 192)
+ROWS = 32 * 224
 GROUPS = 4
 MESH = pl.DeviceIdType.MESH
 
@@ -163,7 +163,7 @@
     res_o, gt_o, f_o,
     wp, bt, alive, xhat1, r1, normed, proj_all, qm, pt, att, xhat2, r2, second, hidden, gp,
     res_v, gt_v, f, cur, nxt, out2, cw, pack, halo_f, halo_out, halo_in,
-    dtot, du, dres, dres_b, datt, dom, dst_, dqkv, w6, *refs
+    dtot, du, dres, dres_b, datt, dom, dst_, dqkv, w5, *refs
 ):
     gs, r0s, hhs, rrs, zs = (refs[GROUPS * i : GROUPS * i + GROUPS] for i in range(5))
     held, sems = refs[5 * GROUPS : 5 * GROUPS + 12], refs[5 * GROUPS + 12 :]
@@ -390,19 +390,22 @@
         stage("b_qkv", b_qkv)
 
     def put(gr, at, matrix):
-        for i in range(6):
-            gs[gr][at + i * D : at + i * D + D, :] = matrix[:, 128 * i : 128 * i + 128].astype(BF16)
-
-    def mlp_terms(b, gr, at):
-        put(gr, at, dot_tn(second[b], du[...]))
-        put(gr, at + 6 * D, dot_tn(dtot[...], hidden[b]))
-
-    def attention_terms(b, gr, at):
-        w6[...] = dot_tn(normed[b], dqkv[...])
+        for i in range(matrix.shape[1] // 128):
+            rows = slice((at + i) * D, (at + i + 1) * D)
+            gs[gr][rows, :] = matrix[:, 128 * i : 128 * i + 128].astype(BF16)
+
+    def mlp_terms(b, gr):
+        put(gr, 0, dot_tn(second[b], du[...]))
+        put(gr, 6, dot_tn(dtot[...], hidden[b]))
         pr = dot_tn(att[b], dres_b[...])
+        put(gr, 12, pr[:, 0:128])
+        w5[b, :, 576:640] = pr[:, 128:D]
+
+    def attention_terms(b, gr):
+        terms = dot_tn(normed[b], dqkv[...])
         for i in range(3):
-            w6[:, 256 * i + D : 256 * i + 256] = pr[:, 64 * i : 64 * i + 64]
-        put(gr, at, w6)
+            w5[b, :, D * i : D * i + D] = terms[:, 256 * i : 256 * i + D]
+        put(gr, 0, w5[b])
 
     def remote(src, dst, send, recv, device):
         return pltpu.make_async_remote_copy(
@@ -421,34 +424,46 @@
         there = pl.ds(pl.multiple_of((1 - core) * rows, 16), rows)
         return remote(gs[gr].at[there], r0s[gr], core_send.at[gr], core_recv.at[gr], sibling())
 
-    def xy_copy(gr, j, slot):
+    def half_at(gr, c):
+        rows = 16 * PIECES[gr]
+        return pl.ds(pl.multiple_of(BASES[gr] + c * rows, 16), rows)
+
+    def xy_copy(gr, k):
+        j = lax.rem(me_xy + k, 16)
         return remote(
-            hhs[gr].at[piece_at(gr, j)], rrs[gr].at[slot],
-            xy_send.at[gr, j], xy_recv.at[gr, slot], xy_dev(j),
+            hhs[gr].at[piece_at(gr, j)], rrs[gr].at[k - 1],
+            xy_send.at[gr], xy_recv.at[gr], xy_dev(j),
         )
 
-    def z_copy(gr, j, slot):
-        return remote(zs[gr].at[slot], zs[gr].at[slot], z_send.at[gr, j], z_recv.at[gr, slot], z_dev(j))
-
-    def ag_copy(gr, j, slot):
-        at = f_at(gr, core, slot)
-        return remote(f.at[at], f.at[at], ag_send.at[gr, j], ag_recv.at[gr, slot], xy_dev(j))
-
-    def fw_copy(gr, j, c):
-        at = f_at(gr, c, j)
-        return remote(f.at[at], f.at[at], fw_send.at[gr, j], fw_recv.at[gr, j], sibling())
-
-    def xy_others(body):
+    def xy_all(gr):
+        every = rrs[gr].at[pl.ds(0, 15)]
+        return remote(every, every, xy_send.at[gr], xy_recv.at[gr], xy_dev(lax.rem(me_xy + 1, 16)))
+
+    def z_copy(gr, k):
+        here = zs[gr].at[zi]
+        return remote(here, here, z_send.at[gr], z_recv.at[gr], z_dev(lax.rem(zi + k, 8)))
+
+    def z_all(gr):
+        every = zs[gr].at[pl.ds(0, 7)]
+        return remote(every, every, z_send.at[gr], z_recv.at[gr], z_dev(lax.rem(zi + 1, 8)))
+
+    def ag_copy(gr, k):
+        here = f.at[f_at(gr, core, me_xy)]
+        return remote(here, here, ag_send.at[gr], ag_recv.at[gr], xy_dev(lax.rem(me_xy + k, 16)))
+
+    def ag_all(gr):
+        every = f.at[pl.ds(BASES[gr], 15 * PIECES[gr])]
+        return remote(every, every, ag_send.at[gr], ag_recv.at[gr], xy_dev(lax.rem(me_xy + 1, 16)))
+
+    def fw_copy(gr, c):
+        half = f.at[half_at(gr, c)]
+        return remote(half, half, fw_send.at[gr], fw_recv.at[gr], sibling())
+
+    def each(count, body):
         def step(k, carry):
-            body(lax.rem(me_xy + k, 16))
+            body(k)
             return carry
-        lax.fori_loop(1, 16, step, 0)
-
-    def z_others(body):
-        def step(k, carry):
-            body(lax.rem(zi + k, 8))
-            return carry
-        lax.fori_loop(1, 8, step, 0)
+        lax.fori_loop(1, count, step, 0)
 
     def sum_0(gr):
         core_copy(gr).start()
@@ -461,51 +476,41 @@
             there = r0s[gr][piece_at(gr, j), :]
             hhs[gr][piece_at(gr, j), :] = (own.astype(F32) + there.astype(F32)).astype(BF16)
 
-        def add_and_send(j):
-            add(j)
-            xy_copy(gr, j, me_xy).start()
-
-        xy_others(add_and_send)
+        def add_and_send(k):
+            add(lax.rem(me_xy + k, 16))
+            xy_copy(gr, k).start()
+
+        each(16, add_and_send)
         add(me_xy)
 
     def sum_2(gr):
-        def step(k, total):
-            j = lax.rem(me_xy + k, 16)
-            xy_copy(gr, me_xy, j).wait_recv()
-            return total + rrs[gr][j].astype(F32)
-
-        own = hhs[gr][piece_at(gr, me_xy), :].astype(F32)
-        zs[gr][zi] = lax.fori_loop(1, 16, step, own).astype(BF16)
-        z_others(lambda j: z_copy(gr, j, zi).start())
+        total = hhs[gr][piece_at(gr, me_xy), :].astype(F32)
+        xy_all(gr).wait_recv()
+        for k in range(15):
+            total = total + rrs[gr][k].astype(F32)
+        zs[gr][zi] = total.astype(BF16)
+        each(8, lambda k: z_copy(gr, k).start())
 
     def sum_3(gr):
-        z_others(lambda j: z_copy(gr, zi, j).wait_recv())
+        z_all(gr).wait_recv()
         total = zs[gr][0].astype(F32)
         for j in range(1, 8):
             total = total + zs[gr][j].astype(F32)
         f[f_at(gr, core, me_xy), :] = total.astype(BF16)
-        xy_others(lambda j: ag_copy(gr, j, me_xy).start())
-        fw_copy(gr, me_xy, core).start()
+        each(16, lambda k: ag_copy(gr, k).start())
 
     def sum_4(gr):
-        def forward(j):
-            ag_copy(gr, me_xy, j).wait_recv()
-            fw_copy(gr, j, core).start()
-        xy_others(forward)
+        ag_all(gr).wait_recv()
+        fw_copy(gr, core).start()
 
     def sum_5(gr):
-        def arrived(j, carry):
-            fw_copy(gr, j, 1 - core).wait_recv()
-            fw_copy(gr, j, core).wait_send()
-            return carry
-        lax.fori_loop(0, 16, arrived, 0)
+        fw_copy(gr, 1 - core).wait_recv()
 
     def sum_sent(gr):
-        def sent(j):
-            xy_copy(gr, j, me_xy).wait_send()
-            ag_copy(gr, j, me_xy).wait_send()
-        xy_others(sent)
-        z_others(lambda j: z_copy(gr, j, zi).wait_send())
+        xy_all(gr).wait_send()
+        z_all(gr).wait_send()
+        ag_all(gr).wait_send()
+        fw_copy(gr, core).wait_send()
 
     def out_copy(gr):
         at = pl.ds(BASES[gr], 32 * PIECES[gr])
@@ -519,7 +524,7 @@
         return pltpu.make_async_copy((res_v, gt_v)[i], (res_o, gt_o)[i], out_sem.at[GROUPS + i])
 
     for gr in range(GROUPS):
-        used = (12, 6)[gr % 2] * D
+        used = (13, 5)[gr % 2] * D
         gs[gr][used:, :] = jnp.zeros((32 * PIECES[gr] - used, 128), BF16)
     loads[0].wait()
     tile_to_windows(tok, cur)
@@ -545,7 +550,7 @@
     halo_start(2, out2, -1)
     halo_finish(0, cw, cur, 1)
     mlp_backward(1, cur, 0, 4)
-    stage("mlp_terms", lambda: mlp_terms(1, 0, 0))
+    stage("mlp_terms", lambda: mlp_terms(1, 0))
     sum_0(0)
     attention_backward(1, 0, 3)
     input_backward(1, cw, 0, 3)
@@ -553,18 +558,18 @@
     sum_1(0)
     attention_backward(1, 3, 4)
     input_backward(1, cw, 3, 4)
-    stage("attention_terms", lambda: attention_terms(1, 1, 0))
+    stage("attention_terms", lambda: attention_terms(1, 1))
     sum_0(1)
     unpack_shift(cw, halo_f, nxt, -1, (0,))
     mlp_backward(0, nxt, 0, 1)
     sum_1(1)
     halo_finish(3, cw, nxt, -1, (1, 2, 3))
     mlp_backward(0, nxt, 1, 4)
-    stage("mlp_terms", lambda: mlp_terms(0, 2, 0))
+    stage("mlp_terms", lambda: mlp_terms(0, 2))
     sum_0(2)
     sum_2(0)
     attention_backward(0, 0, 4, aside)
-    stage("attention_terms", lambda: attention_terms(0, 3, 0))
+    stage("attention_terms", lambda: attention_terms(0, 3))
     sum_0(3)
     input_backward(0, cur, 0, 4)
     sum_1(3)
@@ -618,16 +623,18 @@
         at = BASES[gr] + i * D
         return f[at : at + D, :].astype(F32) * factor
 
-    def attention_out(gr, i, qkv, proj):
-        for n in range(3):
-            two = jnp.concatenate([tile(gr, i + 2 * n), tile(gr, i + 2 * n + 1)], axis=1)
-            qkv[:, D * n : D * n + D] = two[:, 0:D]
-            proj[:, 64 * n : 64 * n + 64] = two[:, D:]
-
-    def mlp_out(gr, i, up, down):
+    def mlp_out(gr, up, down, proj):
         for n in range(6):
-            up[:, 128 * n : 128 * n + 128] = tile(gr, i + n)
-            down[:, 128 * n : 128 * n + 128] = tile(gr, i + 6 + n)
+            up[:, 128 * n : 128 * n + 128] = tile(gr, n)
+            down[:, 128 * n : 128 * n + 128] = tile(gr, n + 6)
+        proj[:, 0:128] = tile(gr, 12)
+
+    def attention_out(gr, qkv, proj):
+        for n in range(4):
+            qkv[:, 128 * n : 128 * n + 128] = tile(gr, n)
+        last = tile(gr, 4)
+        qkv[:, 512:576] = last[:, 0:64]
+        proj[:, 128:D] = last[:, 64:128]
 
     def send(first, count):
         for i in range(first, first + count):
@@ -636,7 +643,7 @@
             copies.append(copy)
 
     parts[0].wait()
-    mlp_out(0, 0, held[6], held[7])
+    mlp_out(0, held[6], held[7], held[5])
     send(6, 2)
     for i, (held_f, out_f) in enumerate(((res_v, res_o), (gt_v, gt_o))):
         fields[i].wait()
@@ -644,13 +651,13 @@
         copy.start()
         copies.append(copy)
     parts[1].wait()
-    attention_out(1, 0, held[4], held[5])
+    attention_out(1, held[4], held[5])
     send(4, 2)
     parts[2].wait()
-    mlp_out(2, 0, held[2], held[3])
+    mlp_out(2, held[2], held[3], held[1])
     send(2, 2)
     parts[3].wait()
-    attention_out(3, 0, held[0], held[1])
+    attention_out(3, held[0], held[1])
     send(0, 2)
     for copy in copies:
         copy.wait()
@@ -707,7 +714,7 @@
         pltpu.VMEM((4, STACK, D), BF16),
         pltpu.VMEM((4, WIN, STACK), BF16),
         pltpu.VMEM((576, 768), BF16),
-        pltpu.VMEM((D, 768), F32),
+        pltpu.VMEM((2, D, 640), F32),
         *[pltpu.VMEM((32 * r, 128), BF16) for r in PIECES],
         *[pltpu.VMEM((16 * r, 128), BF16) for r in PIECES],
         *[pltpu.VMEM((16 * r, 128), BF16) for r in PIECES],
@@ -716,10 +723,10 @@
         *[pltpu.VMEM(a.shape, BF16) for a in big],
         dma(4, 3), dma(4, 3),
         dma(GROUPS), dma(GROUPS),
-        dma(GROUPS, 16), dma(GROUPS, 16),
-        dma(GROUPS, 8), dma(GROUPS, 8),
-        dma(GROUPS, 16), dma(GROUPS, 16),
-        dma(GROUPS, 16), dma(GROUPS, 16),
+        dma(GROUPS), dma(GROUPS),
+        dma(GROUPS), dma(GROUPS),
+        dma(GROUPS), dma(GROUPS),
+        dma(GROUPS), dma(GROUPS),
         dma(GROUPS + 2), dma(12),
     ]
     res, gt, f = pl.pallas_call(

time: 70.6 us -> 64.2 us (0.909)
  Pallas kernels: 69.6 us -> 63.2 us
    pallas_call x1, Pallas kernels: 66.2 us -> 59.9 us  [body(): pl.pallas_call(megakernel, out_shape=(tile, tile, jax.ShapeDtypeStruct((R...]
where the time goes in v3:
time: 64.2 us; the launch traced here: 64 us
  Pallas kernels  63.2 us (98%)
  between operations  0.82 us (1%)
    pallas_call x1, Pallas kernels, body(): pl.pallas_call(megakernel, out_shape=(tile, tile, jax.ShapeDtypeStruct((R...  59.9 us
    pallas_call x1, Pallas kernels, body(): pl.pallas_call(functools.partial(unpack_kernel, 1.0 / math.sqrt(256.0 * 5...  3.31 us

profile of v3, /device:TPU:1, one launch (start us, length us, event | category | flops | bytes accessed | tf_op | source)
XLA Modules:
  0.0 64.0 jit_solution(7326973139182151016)
XLA Ops:
  0.6 59.9 %shard_map.231 = (bf16[24,24,192]{2,1,0:T(8,128)(2,1)}, bf16[24,24,192]{2,1,0:T(8,128)(2,1)}, bf16[7168,128]{1,0:T(8,128)(2,1)}) custom-call(f32[192]{0:T(256)} %ga1.1, f32[192]{0:T(256)} %gm1.1, f32[192]{0:T(256)} %ga2.1, f32[192]{0:T(256)} %gm2.1, bf16[24,24,192]{2,1,0:T(8,128)(2,1)} %bitcast.12, bf16[24,24,192]{2,1,0:T(8,128)(2,1)} %bitcast.13, ...), custom_call_target="tpu_custom_call" | custom-call | tf_op jit(solution)/shard_map/pallas_call | solution.py:732
  60.6 3.3 %shard_map.232 = (bf16[24,24,192]{2,1,0:T(8,128)(2,1)}, bf16[24,24,192]{2,1,0:T(8,128)(2,1)}, f32[192,576]{1,0:T(8,128)}, f32[192,192]{1,0:T(8,128)}, f32[192,76...) custom-call(bf16[7168,128]{1,0:T(8,128)(2,1)} %get-tuple-element.23., ...), custom_call_target="tpu_custom_call" | custom-call | tf_op jit(solution)/shard_map/pallas_call | solution.py:750

commit v4 on v3

--- a/solution.py
+++ b/solution.py
@@ -114,17 +114,18 @@
     return ((row // 6) * 2 + col // 12) * WIN + level * 72 + (row % 6) * 12 + col % 12
 
 
-def pack_halo(src, pack, out, row0, row1, col0, col1):
-    at = 0
-    for rows, cols in ((row0, col1), (row1, col0), (row1, col1)):
+def pack_halo(src, pack, out, row0, row1, col0, col1, parts):
+    for part in parts:
+        rows, cols = ((row0, col1), (row1, col0), (row1, col1))[part]
+        first, count = HALO_PARTS[part]
+        at = first
         for level in range(2):
             for row in rows:
                 for col in cols:
                     p = place(level, row, col)
                     pack[at : at + 6, :] = src[p : p + 6, :]
                     at += 6
-        at = (at + 15) // 16 * 16
-    out[...] = pack[...].astype(BF16)
+        out[first : first + count, :] = pack[first : first + count, :].astype(BF16)
 
 
 HALO_ROWS = 112 + 112 + 48
@@ -230,12 +231,13 @@
             device_id_type=MESH,
         )
 
-    def halo_start(x, src, step):
+    def halo_start(x, src, step, parts=(0, 1, 2)):
         if step > 0:
-            pack_halo(src, pack, halo_out.at[x], range(0, 9), range(9, 12), (0, 6, 12), (18,))
+            where = (range(0, 9), range(9, 12), (0, 6, 12), (18,))
         else:
-            pack_halo(src, pack, halo_out.at[x], range(3, 12), range(0, 3), (6, 12, 18), (0,))
-        for part in range(3):
+            where = (range(3, 12), range(0, 3), (6, 12, 18), (0,))
+        pack_halo(src, pack, halo_out.at[x], *where, parts)
+        for part in parts:
             halo_copy(x, part, step).start()
 
     def halo_finish(x, src, dst, step, windows=(0, 1, 2, 3)):
@@ -519,6 +521,8 @@
     def aside(w):
         if w == 1:
             sum_1(2)
+        if w == 2:
+            sum_2(0)
 
     def field_copy(i):
         return pltpu.make_async_copy((res_v, gt_v)[i], (res_o, gt_o)[i], out_sem.at[GROUPS + i])
@@ -531,15 +535,16 @@
     loads[2].wait()
     loads[6].wait()
     stage("prepare", lambda: prepare(0))
+    for i in (3, 4, 5):
+        loads[i].wait()
+    block_forward(0, cur, nxt, 2, 4)
+    pl.semaphore_wait(barrier, 29)
+    halo_start(1, nxt, 1, (1, 2))
+    block_forward(0, cur, nxt, 0, 2)
+    halo_start(1, nxt, 1, (0,))
     loads[1].wait()
     tile_to_windows(ct, cw)
-    pl.semaphore_wait(barrier, 29)
     halo_start(0, cw, 1)
-    for i in (3, 4, 5):
-        loads[i].wait()
-    block_forward(0, cur, nxt, 1, 4)
-    halo_start(1, nxt, 1)
-    block_forward(0, cur, nxt, 0, 1)
     for i in (7, 8, 9, 10, 11):
         loads[i].wait()
     stage("prepare", lambda: prepare(1))
@@ -552,9 +557,12 @@
     mlp_backward(1, cur, 0, 4)
     stage("mlp_terms", lambda: mlp_terms(1, 0))
     sum_0(0)
-    attention_backward(1, 0, 3)
-    input_backward(1, cw, 0, 3)
-    halo_start(3, cw, -1)
+    attention_backward(1, 0, 2)
+    input_backward(1, cw, 0, 2)
+    halo_start(3, cw, -1, (1, 2))
+    attention_backward(1, 2, 3)
+    input_backward(1, cw, 2, 3)
+    halo_start(3, cw, -1, (0,))
     sum_1(0)
     attention_backward(1, 3, 4)
     input_backward(1, cw, 3, 4)
@@ -567,7 +575,6 @@
     mlp_backward(0, nxt, 1, 4)
     stage("mlp_terms", lambda: mlp_terms(0, 2))
     sum_0(2)
-    sum_2(0)
     attention_backward(0, 0, 4, aside)
     stage("attention_terms", lambda: attention_terms(0, 3))
     sum_0(3)
@@ -581,8 +588,8 @@
     field_copy(0).start()
     sum_3(0)
     sum_2(2)
+    sum_2(3)
     sum_3(1)
-    sum_2(3)
     sum_4(0)
     sum_3(2)
     sum_4(1)

time: 64.2 us -> 63.3 us (0.986)
  Pallas kernels: 63.2 us -> 62.4 us
    pallas_call x1, Pallas kernels: 59.9 us -> 59.1 us  [body(): pl.pallas_call(megakernel, out_shape=(tile, tile, jax.ShapeDtypeStruct((R...]
where the time goes in v4:
time: 63.3 us; the launch traced here: 63.2 us
  Pallas kernels  62.4 us (99%)
  between operations  0.82 us (1%)
    pallas_call x1, Pallas kernels, body(): pl.pallas_call(megakernel, out_shape=(tile, tile, jax.ShapeDtypeStruct((R...  59.1 us
    pallas_call x1, Pallas kernels, body(): pl.pallas_call(functools.partial(unpack_kernel, 1.0 / math.sqrt(256.0 * 5...  3.31 us

profile of v4, /device:TPU:1, one launch (start us, length us, event | category | flops | bytes accessed | tf_op | source)
XLA Modules:
  0.0 63.2 jit_solution(7570319570872595027)
XLA Ops:
  0.6 59.1 %shard_map.231 = (bf16[24,24,192]{2,1,0:T(8,128)(2,1)}, bf16[24,24,192]{2,1,0:T(8,128)(2,1)}, bf16[7168,128]{1,0:T(8,128)(2,1)}) custom-call(f32[192]{0:T(256)} %ga1.1, f32[192]{0:T(256)} %gm1.1, f32[192]{0:T(256)} %ga2.1, f32[192]{0:T(256)} %gm2.1, bf16[24,24,192]{2,1,0:T(8,128)(2,1)} %bitcast.12, bf16[24,24,192]{2,1,0:T(8,128)(2,1)} %bitcast.13, ...), custom_call_target="tpu_custom_call" | custom-call | tf_op jit(solution)/shard_map/pallas_call | solution.py:739
  59.8 3.3 %shard_map.232 = (bf16[24,24,192]{2,1,0:T(8,128)(2,1)}, bf16[24,24,192]{2,1,0:T(8,128)(2,1)}, f32[192,576]{1,0:T(8,128)}, f32[192,192]{1,0:T(8,128)}, f32[192,76...) custom-call(bf16[7168,128]{1,0:T(8,128)(2,1)} %get-tuple-element.23., ...), custom_call_target="tpu_custom_call" | custom-call | tf_op jit(solution)/shard_map/pallas_call | solution.py:757

commit v5 on v4

--- a/solution.py
+++ b/solution.py
@@ -521,8 +521,6 @@
     def aside(w):
         if w == 1:
             sum_1(2)
-        if w == 2:
-            sum_2(0)
 
     def field_copy(i):
         return pltpu.make_async_copy((res_v, gt_v)[i], (res_o, gt_o)[i], out_sem.at[GROUPS + i])
@@ -575,6 +573,7 @@
     mlp_backward(0, nxt, 1, 4)
     stage("mlp_terms", lambda: mlp_terms(0, 2))
     sum_0(2)
+    sum_2(0)
     attention_backward(0, 0, 4, aside)
     stage("attention_terms", lambda: attention_terms(0, 3))
     sum_0(3)
@@ -588,8 +587,8 @@
     field_copy(0).start()
     sum_3(0)
     sum_2(2)
+    sum_3(1)
     sum_2(3)
-    sum_3(1)
     sum_4(0)
     sum_3(2)
     sum_4(1)

time: 63.3 us -> 62.9 us (level)
  no operation moved by 1% of the time
where the time goes in v5:
time: 62.9 us; the launch traced here: 62.7 us
  Pallas kernels  61.9 us (98%)
  between operations  0.82 us (1%)
    pallas_call x1, Pallas kernels, body(): pl.pallas_call(megakernel, out_shape=(tile, tile, jax.ShapeDtypeStruct((R...  58.6 us
    pallas_call x1, Pallas kernels, body(): pl.pallas_call(functools.partial(unpack_kernel, 1.0 / math.sqrt(256.0 * 5...  3.31 us

profile of v5, /device:TPU:1, one launch (start us, length us, event | category | flops | bytes accessed | tf_op | source)
XLA Modules:
  0.0 62.7 jit_solution(8322395821806057077)
XLA Ops:
  0.6 58.6 %shard_map.231 = (bf16[24,24,192]{2,1,0:T(8,128)(2,1)}, bf16[24,24,192]{2,1,0:T(8,128)(2,1)}, bf16[7168,128]{1,0:T(8,128)(2,1)}) custom-call(f32[192]{0:T(256)} %ga1.1, f32[192]{0:T(256)} %gm1.1, f32[192]{0:T(256)} %ga2.1, f32[192]{0:T(256)} %gm2.1, bf16[24,24,192]{2,1,0:T(8,128)(2,1)} %bitcast.12, bf16[24,24,192]{2,1,0:T(8,128)(2,1)} %bitcast.13, ...), custom_call_target="tpu_custom_call" | custom-call | tf_op jit(solution)/shard_map/pallas_call | solution.py:738
  59.3 3.3 %shard_map.232 = (bf16[24,24,192]{2,1,0:T(8,128)(2,1)}, bf16[24,24,192]{2,1,0:T(8,128)(2,1)}, f32[192,576]{1,0:T(8,128)}, f32[192,192]{1,0:T(8,128)}, f32[192,76...) custom-call(bf16[7168,128]{1,0:T(8,128)(2,1)} %get-tuple-element.23., ...), custom_call_target="tpu_custom_call" | custom-call | tf_op jit(solution)/shard_map/pallas_call | solution.py:756
